TPU v7x, 256 devices: a whole 4x4x8 slice. The times are simulated.
256 devices in a mesh: grp: 8 (over z), lat: 32 (over y, x, core).
Axes of the slice: x: 4, y: 4, z: 8, core: 2. Of those that a mesh axis runs over, the one named last changes fastest.
Arguments:
- state: bfloat16 [16, 512, 4096], P(None, ('grp', 'lat')), may hold values from -6 to 6
- dep_row: int32 [512, 4096], P(('grp', 'lat')), may hold values from 0 to 510, as said below
- dep_col: int32 [512, 4096], P(('grp', 'lat')), may hold values from 0 to 4095, as said below
- row_weight: float32 [512, 4096], P(('grp', 'lat')), may hold values from 0 to 1
- col_weight: float32 [512, 4096], P(('grp', 'lat')), may hold values from 0 to 1
- wave_of: int32 [1024], replicated, may hold values from 0 to 1023, as said below
- legendre: bfloat16 [1024, 2, 256, 512], P(('grp', 'lat')), as said below
- gamma: float32 [16], replicated, may hold values from 0.3 to 30
- rad_place: int32 [256, 1024], P(('grp', 'lat')), may hold values from 0 to 32767, as said below
- optics: bfloat16 [262144, 16], P(('grp', 'lat')), may hold values from 0.049804688 to 2
- kabs: float32 [16, 128], replicated, may hold values from 0.02 to 0.3
- planck_weight: float32 [16, 128], replicated, may hold values from -1.5 to 1.5
- kdown: float32 [128, 16], replicated, may hold values from -0.5 to 0.5
Outputs:
- new_state: bfloat16 [16, 512, 4096], P(None, ('grp', 'lat'))
Inputs may be any that keep to these rules, and one draw needn't show every extreme that they name: dep_row[i, j] lies between i - 2 and i + 1. (dep_col[i, j] - j) mod 4096 is one of 0, 1, 2, 4094, 4095. `wave_of`: every wavenumber once; slots 4 d to 4 d + 3 hold pairs m, 1023 - m for wavenumbers m below 512. `rad_place`: a value is owner * 1024 + slot with owner below 32 and slot below 1024; within the coarse rows of one group of 32 devices every value appears once; the 1024 coarse columns of one device's rows name one owner at most 48 times, and some device names some owner exactly 48 times. `legendre`: zero where 2 h + p exceeds 1023 minus the slot's wavenumber.
All inputs are finite; a program needn't handle non-finite values.
Results may differ from a plain program's by a relative error of at most 0.0078.
Values may be sent and summed in bfloat16 or wider, within the bound.
A program may use at most 128 MiB of HBM per device.

v0:
```python
import functools
import math

import jax
import jax.numpy as jnp
from jax import lax
from jax.experimental import pallas as pl
from jax.experimental.pallas import tpu as pltpu
from jax.sharding import PartitionSpec as P

F32 = jnp.float32
BF16 = jnp.bfloat16
RADIX = 32
HALF = RADIX // 2 + 1
VMEM_LIMIT = 48 * 1024 * 1024
MESH = pl.DeviceIdType.MESH


def cplx(angle_num, angle_den):
    turn = 2.0 * math.pi * angle_num / angle_den
    return math.cos(turn), math.sin(turn)


def real_fft(planes):
    count = len(planes)
    if count == 2:
        return [(planes[0] + planes[1], None), (planes[0] - planes[1], None)]
    even = real_fft(planes[0::2])
    odd = real_fft(planes[1::2])
    half = count // 2
    out = []
    for k in range(half + 1):

        def pick(spec):
            kk = k % half
            if kk <= half // 2:
                return spec[kk]
            re, im = spec[half - kk]
            return re, (None if im is None else -im)

        er, ei = pick(even)
        orr, oi = pick(odd)
        c, s = cplx(k, count)
        if k == 0:
            out.append((er + orr, None))
        elif k == half:
            out.append((er - orr, None))
        elif 4 * k == count:
            out.append((er, -orr))
        else:
            if oi is None:
                tr, ti = c * orr, -s * orr
            else:
                tr, ti = c * orr + s * oi, c * oi - s * orr
            out.append((er + tr, ti if ei is None else ei + ti))
    return out


def real_ifft(spec):
    half = len(spec) - 1
    count = 2 * half
    if count == 2:
        return [spec[0][0] + spec[1][0], spec[0][0] - spec[1][0]]
    even, odd = [], []
    for k in range(half // 2 + 1):
        xr, xi = spec[k]
        yr, yi = spec[half - k]
        if k == 0:
            even.append((xr + yr, None))
            odd.append((xr - yr, None))
        elif 2 * k == half:
            even.append((xr + xr, None))
            odd.append((-(xi + xi), None))
        else:
            even.append((xr + yr, xi - yi))
            dr, di = xr - yr, xi + yi
            c, s = cplx(k, count)
            odd.append((c * dr - s * di, c * di + s * dr))
    ev, od = real_ifft(even), real_ifft(odd)
    return [plane for pair in zip(ev, od) for plane in pair]


def forward_kernel(
    row_start_ref, prev_ref, own_ref, next_ref, row_ref, col_ref, rw_ref, cw_ref,
    table_ref, fold_ref, out_ref, rows_ref, departed_ref, z_ref, ft_ref,
):
    lon = own_ref.shape[2]
    levels = own_ref.shape[1]
    for i in range(2):
        rows_ref[i] = prev_ref[i].astype(F32)
        rows_ref[2 + i] = own_ref[i].astype(F32)
        rows_ref[4 + i] = next_ref[i].astype(F32)
    sub = lax.broadcasted_iota(jnp.int32, (8, lon), 0) - 2
    lon_ids = lax.broadcasted_iota(jnp.int32, (1, lon), 1)
    start = row_start_ref[0]
    for i in range(2):
        rel_row = row_ref[i : i + 1, :] - (start + i)
        rel_col = (col_ref[i : i + 1, :] - lon_ids + 2) & (lon - 1)
        rel_col = rel_col - 2
        a = rw_ref[i : i + 1, :]
        b = cw_ref[i : i + 1, :]
        row_w = jnp.where(rel_row == sub, 1.0 - a, 0.0) + jnp.where(rel_row == sub - 1, a, 0.0)
        col_w = jnp.where(rel_col == sub, 1.0 - b, 0.0) + jnp.where(rel_col == sub - 1, b, 0.0)
        shifted = [
            row_w if dc == 0 else pltpu.roll(row_w, dc % lon, 1) for dc in range(-2, 4)
        ]
        for h in range(levels // 8):
            total = None
            for dc in range(-2, 4):
                mixed = None
                for dr in range(5):
                    term = shifted[dc + 2][dr : dr + 1, :] * rows_ref[i + dr, 8 * h : 8 * h + 8, :]
                    mixed = term if mixed is None else mixed + term
                if dc != 0:
                    mixed = pltpu.roll(mixed, (-dc) % lon, 1)
                term = col_w[dc + 2 : dc + 3, :] * mixed
                total = term if total is None else total + term
            departed_ref[i, 8 * h : 8 * h + 8, :] = total
    for i in range(2):
        planes = [
            departed_ref[i, :, 128 * j : 128 * j + 128].astype(BF16).astype(F32)
            for j in range(RADIX)
        ]
        for k, (re, im) in enumerate(real_fft(planes)):
            at = 2 * levels * k + levels * i
            z_ref[at : at + levels, 0:128] = re.astype(BF16)
            z_ref[at : at + levels, 128:256] = (
                jnp.zeros((levels, 128), BF16) if im is None else im.astype(BF16)
            )
    scale = math.sqrt(2.0 / lon)
    r = 2 * levels
    for c in range(8):
        prod = lax.dot_general(
            z_ref[...], table_ref[256 * c : 256 * c + 256, :],
            (((1,), (1,)), ((), ())), preferred_element_type=F32,
        )
        fold = fold_ref[c // 2 : c // 2 + 1, :]
        got = prod[0:r]
        for k in range(1, HALF):
            got = jnp.where(fold == k, prod[r * k : r * k + r], got)
        got = got * scale
        for i in range(2):
            ft_ref[128 * i + 16 * c : 128 * i + 16 * c + 16, :] = got[16 * i : 16 * i + 16]
    swapped = jnp.transpose(ft_ref[...])
    parts = [swapped[:, 128 * i : 128 * i + 128].reshape(32, 1, 8, 128) for i in range(2)]
    out_ref[...] = jnp.concatenate(parts, axis=1).reshape(512, 128).astype(BF16)


def inverse_kernel(got_ref, table_ref, fold_ref, heat_ref, out_ref, e_ref):
    levels = heat_ref.shape[0]
    lon = out_ref.shape[2]
    r = 2 * levels
    rows = got_ref[...].astype(F32).reshape(32, 2, 8, 128)
    turned = [jnp.transpose(rows[:, i].reshape(256, 128)) for i in range(2)]
    for c in range(8):
        piece = jnp.concatenate([t[16 * c : 16 * c + 16] for t in turned], axis=0)
        fold = fold_ref[c // 2 : c // 2 + 1, :]
        for k in range(HALF):
            e_ref[r * k : r * k + r, 256 * c : 256 * c + 256] = jnp.where(
                fold == k, piece, 0.0
            ).astype(BF16)
    waves = jnp.dot(e_ref[...], table_ref[...], preferred_element_type=F32)
    low = lax.broadcasted_iota(jnp.int32, (128, 512), 0)
    high = lax.broadcasted_iota(jnp.int32, (128, 512), 1)
    spread = jnp.where(low == high // 4, 1.0, 0.0).astype(BF16)
    heat = [
        jnp.dot(heat_ref[:, 128 * b : 128 * b + 128], spread, preferred_element_type=F32)
        for b in range(lon // 512)
    ]
    scale = 0.5 * math.sqrt(2.0 / lon)
    for i in range(2):
        spec = []
        for k in range(HALF):
            at = r * k + levels * i
            block = waves[at : at + levels]
            re, im = block[:, 0:128], block[:, 128:256]
            if k in (0, HALF - 1):
                spec.append((re + re, None))
            else:
                spec.append((re, im))
        for j, plane in enumerate(real_ifft(spec)):
            warm = heat[j // 4][:, 128 * (j % 4) : 128 * (j % 4) + 128]
            out_ref[i, :, 128 * j : 128 * j + 128] = (plane * scale + warm).astype(BF16)


def radiation_kernel(own_ref, place_ref, optics_ref, kabs_ref, planck_ref, kdown_ref, out_ref):
    levels = own_ref.shape[1]
    lon = own_ref.shape[2]
    cols = lon // 4
    high = lax.broadcasted_iota(jnp.int32, (512, 128), 0)
    low = lax.broadcasted_iota(jnp.int32, (512, 128), 1)
    pool = jnp.where(high // 4 == low, 1.0, 0.0).astype(BF16)
    temps = []
    for b in range(lon // 512):
        part = None
        for e in range(2):
            term = jnp.dot(
                own_ref[e, :, 512 * b : 512 * b + 512], pool, preferred_element_type=F32
            )
            part = term if part is None else part + term
        temps.append(part)
    temps = (jnp.concatenate(temps, axis=1) * 0.125).astype(BF16).astype(F32)
    place = place_ref[...]
    slot = place & (cols - 1)
    owner = place // cols
    depth_all = None
    for b in range(cols // 256):
        ids = lax.broadcasted_iota(jnp.int32, (256, cols), 0) + 256 * b
        hot = jnp.where(ids == slot, 1.0, 0.0).astype(BF16)
        term = jnp.dot(
            optics_ref[:, 256 * b : 256 * b + 256], hot, preferred_element_type=F32
        )
        depth_all = term if depth_all is None else depth_all + term
    depth = depth_all[0:levels]
    for o in range(1, optics_ref.shape[0] // levels):
        depth = jnp.where(owner == o, depth_all[levels * o : levels * o + levels], depth)
    best = lax.Precision.HIGHEST
    emission = 1.0 + jnp.tanh(temps)
    optical = jnp.dot(kabs_ref[...], depth, precision=best, preferred_element_type=F32)
    source = jnp.dot(planck_ref[...], emission, precision=best, preferred_element_type=F32)
    out_ref[...] = jnp.dot(
        kdown_ref[...], jnp.exp(-optical) * source, precision=best, preferred_element_type=F32
    ).astype(BF16)


def one_hot(shape, want):
    rows = lax.broadcasted_iota(jnp.int32, shape, 0)
    cols = lax.broadcasted_iota(jnp.int32, shape, 1)
    return jnp.where(want(rows) == cols, 1.0, 0.0).astype(BF16)


def lat_first(row):
    return (row % 32) * 16 + ((row // 32) % 2) * 8 + row // 64


def group_first(row):
    return (row % 8) * 64 + ((row // 8) % 2) * 32 + row // 16


def natural(row):
    return (row // 64) * 64 + (row % 2) * 32 + (row % 64) // 2


def unnatural(row):
    return (row // 64) * 64 + (row % 32) * 2 + (row % 64) // 32


def permuted(matrix, data):
    return jnp.dot(matrix, data, preferred_element_type=F32)


def legendre_step(north_in, south_in, table_ref, gamma_ref, waves_ref, turn, trunc):
    to_north, to_south, from_north, from_south = turn
    north = permuted(to_north, north_in)
    south = permuted(to_south, south_in)
    sym = jnp.transpose(north + south).astype(BF16)
    anti = jnp.transpose(north - south).astype(BF16)
    half_degree = table_ref.shape[3]
    steps = lax.broadcasted_iota(jnp.int32, (1, half_degree), 1)
    norm = float(trunc * (trunc + 1))
    gamma = gamma_ref[...]
    even_rows, odd_rows = [], []
    for s in range(4):
        pair = []
        for p, source in enumerate((sym, anti)):
            table = table_ref[s, p]
            spec = jnp.dot(source[32 * s : 32 * s + 32], table, preferred_element_type=F32)
            degree = (waves_ref[s] + 2 * steps + p).astype(F32)
            divisor = 1.0 + gamma * (degree * (degree + 1.0)) / norm
            solved = (spec / divisor).astype(BF16)
            pair.append(
                4.0
                * lax.dot_general(
                    solved, table, (((1,), (1,)), ((), ())), preferred_element_type=F32
                )
            )
        even_rows.append(pair[0])
        odd_rows.append(pair[1])
    even = jnp.concatenate(even_rows, axis=0)
    odd = jnp.concatenate(odd_rows, axis=0)
    north = jnp.transpose(even + odd).astype(BF16)
    south = jnp.transpose(even - odd).astype(BF16)
    return permuted(from_north, north).astype(BF16), permuted(from_south, south).astype(BF16)


def middle_kernel(
    trunc, sent_ref, table_ref, gamma_ref, waves_ref, out_ref,
    got1, send2, got2, send3, got3, send4,
    send_lat, recv_lat, send_grp, recv_grp, send_grp2, recv_grp2, send_lat2, recv_lat2,
):
    g = lax.axis_index("grp")
    a = lax.axis_index("lat")
    barrier = pltpu.get_barrier_semaphore()

    @pl.loop(1, 32)
    def _(k):
        pl.semaphore_signal(
            barrier, inc=1, device_id=(g, lax.rem(a + k, 32)), device_id_type=MESH
        )

    @pl.loop(1, 8)
    def _(k):
        pl.semaphore_signal(
            barrier, inc=1, device_id=(lax.rem(g + k, 8), a), device_id_type=MESH
        )

    pl.semaphore_wait(barrier, 38)

    def exchange(source, target, block, send_sems, recv_sems, count, mine, peer_of):
        def copy(k):
            peer = lax.rem(mine + k, count)
            return pltpu.make_async_remote_copy(
                src_ref=source.at[pl.ds(pl.multiple_of(peer * block, block), block)],
                dst_ref=target.at[pl.ds(pl.multiple_of(mine * block, block), block)],
                send_sem=send_sems.at[k],
                recv_sem=recv_sems.at[k],
                device_id=peer_of(peer),
                device_id_type=MESH,
            )

        def arrival(k):
            peer = lax.rem(mine + count - k, count)
            return pltpu.make_async_remote_copy(
                src_ref=source.at[pl.ds(pl.multiple_of(peer * block, block), block)],
                dst_ref=target.at[pl.ds(pl.multiple_of(peer * block, block), block)],
                send_sem=send_sems.at[k],
                recv_sem=recv_sems.at[k],
                device_id=peer_of(peer),
                device_id_type=MESH,
            )

        @pl.loop(1, count)
        def _(k):
            copy(k).start()

        here = pl.ds(pl.multiple_of(mine * block, block), block)
        target[here, :] = source[here, :]

        def finish():
            @pl.loop(1, count)
            def _(k):
                copy(k).wait_send()
                arrival(k).wait_recv()

        return finish

    def over_lat(peer):
        return (g, peer)

    def over_grp(peer):
        return (peer, a)

    done = exchange(sent_ref, got1, 16, send_lat, recv_lat, 32, a, over_lat)
    to_group = one_hot((512, 512), lat_first)
    done()
    send2[...] = permuted(to_group, got1[...]).astype(BF16)
    done = exchange(send2, got2, 64, send_grp, recv_grp, 8, g, over_grp)
    turn = (
        one_hot((256, 256), natural),
        one_hot((256, 256), lambda row: natural(255 - row)),
        one_hot((256, 256), unnatural),
        one_hot((256, 256), lambda row: 255 - unnatural(row)),
    )
    done()
    north, south = legendre_step(
        got2[0:256, :], got2[256:512, :], table_ref, gamma_ref, waves_ref, turn, trunc
    )
    send3[0:256, :] = north
    send3[256:512, :] = south
    done = exchange(send3, got3, 64, send_grp2, recv_grp2, 8, g, over_grp)
    to_lat = one_hot((512, 512), group_first)
    done()
    send4[...] = permuted(to_lat, got3[...]).astype(BF16)
    exchange(send4, out_ref, 16, send_lat2, recv_lat2, 32, a, over_lat)()


def vmem(count):
    return [pl.BlockSpec(memory_space=pltpu.VMEM)] * count


def shards(
    state, dep_row, dep_col, row_weight, col_weight, wave_of, legendre, gamma,
    rad_place, optics, kabs, planck_weight, kdown,
):
    levels, lat_rows, lon = state.shape
    groups = lax.axis_size("grp")
    owners = lax.axis_size("lat")
    total_waves = wave_of.shape[0]
    dev_index = lax.axis_index("grp") * owners + lax.axis_index("lat")
    params = pltpu.CompilerParams(vmem_limit_bytes=VMEM_LIMIT)

    own = jnp.transpose(state, (1, 0, 2))
    devices = groups * owners
    up = [(i, i + 1) for i in range(devices - 1)]
    down = [(i + 1, i) for i in range(devices - 1)]
    before = lax.ppermute(own, ("grp", "lat"), up)
    after = lax.ppermute(own, ("grp", "lat"), down)
    optics_all = lax.all_gather(jnp.transpose(optics), "lat", axis=0, tiled=True)

    waves = wave_of.reshape(groups, owners, 4).transpose(2, 1, 0).reshape(4, devices)
    class_of = waves % RADIX
    fold = jnp.minimum(class_of, RADIX - class_of)
    points = waves[:, :, None] * jnp.arange(128, dtype=jnp.int32)[None, None, :] % lon
    angles = points.astype(F32) * (2.0 * math.pi / lon)
    cosine, sine = jnp.cos(angles), jnp.sin(angles)
    side = jnp.where(class_of > RADIX // 2, -1.0, 1.0)[:, :, None]
    table = jnp.stack(
        [
            jnp.concatenate([cosine, side * sine], axis=2),
            jnp.concatenate([-sine, side * cosine], axis=2),
        ],
        axis=1,
    ).astype(BF16).reshape(8 * devices, 256)

    outbound = pl.pallas_call(
        forward_kernel,
        out_shape=jax.ShapeDtypeStruct((2 * devices, 128), BF16),
        in_specs=[pl.BlockSpec(memory_space=pltpu.SMEM)] + vmem(9),
        out_specs=pl.BlockSpec(memory_space=pltpu.VMEM),
        scratch_shapes=[
            pltpu.VMEM((6, levels, lon), F32),
            pltpu.VMEM((2, levels, lon), F32),
            pltpu.VMEM((HALF * 2 * levels, 256), BF16),
            pltpu.VMEM((256, 256), F32),
        ],
        compiler_params=params,
        name="interp_fourier",
    )(
        (dev_index * lat_rows).astype(jnp.int32).reshape(1), before, own, after,
        dep_row, dep_col, row_weight, col_weight, table, fold,
    )

    heat = pl.pallas_call(
        radiation_kernel,
        out_shape=jax.ShapeDtypeStruct((levels, lon // 4), BF16),
        in_specs=vmem(6),
        out_specs=pl.BlockSpec(memory_space=pltpu.VMEM),
        compiler_params=params,
        name="radiation",
    )(own, rad_place, optics_all, kabs.T, planck_weight.T, kdown.T)

    my_waves = lax.dynamic_slice_in_dim(wave_of, dev_index * 4, 4)
    rows = 2 * devices
    inbound = pl.pallas_call(
        functools.partial(middle_kernel, total_waves - 1),
        out_shape=jax.ShapeDtypeStruct((rows, 128), BF16),
        in_specs=vmem(3) + [pl.BlockSpec(memory_space=pltpu.SMEM)],
        out_specs=pl.BlockSpec(memory_space=pltpu.VMEM),
        scratch_shapes=[pltpu.VMEM((rows, 128), BF16)] * 6
        + [
            pltpu.SemaphoreType.DMA((32,)),
            pltpu.SemaphoreType.DMA((32,)),
            pltpu.SemaphoreType.DMA((8,)),
            pltpu.SemaphoreType.DMA((8,)),
            pltpu.SemaphoreType.DMA((8,)),
            pltpu.SemaphoreType.DMA((8,)),
            pltpu.SemaphoreType.DMA((32,)),
            pltpu.SemaphoreType.DMA((32,)),
        ],
        compiler_params=pltpu.CompilerParams(
            vmem_limit_bytes=VMEM_LIMIT, collective_id=0, has_side_effects=True
        ),
        name="legendre_exchange",
    )(outbound, legendre, jnp.tile(gamma, 2)[:, None], my_waves)

    result = pl.pallas_call(
        inverse_kernel,
        out_shape=jax.ShapeDtypeStruct((lat_rows, levels, lon), BF16),
        in_specs=vmem(4),
        out_specs=pl.BlockSpec(memory_space=pltpu.VMEM),
        scratch_shapes=[pltpu.VMEM((HALF * 2 * levels, 8 * devices), BF16)],
        compiler_params=params,
        name="inverse_fourier",
    )(inbound, table, fold, heat)
    return jnp.transpose(result, (1, 0, 2))


def solution(mesh):
    return jax.shard_map(
        shards,
        mesh=mesh,
        in_specs=(
            P(None, ("grp", "lat"), None),
            P(("grp", "lat"), None),
            P(("grp", "lat"), None),
            P(("grp", "lat"), None),
            P(("grp", "lat"), None),
            P(),
            P(("grp", "lat"), None, None, None),
            P(),
            P(("grp", "lat"), None),
            P(("grp", "lat"), None),
            P(),
            P(),
            P(),
        ),
        out_specs=P(None, ("grp", "lat"), None),
        check_vma=False,
    )
```

profile of v0, /device:TPU:1, one launch (start us, length us, event | category | flops | bytes accessed | tf_op | source)
XLA Modules:
  0.0 84.1 jit_solution(3726615819837914985)
XLA Ops:
  6.5 0.0 all-gather.2.cloned.1.call-start
  6.5 0.7 all-gather.2.cloned.1.call-update
  7.3 1.1 %copy.28 = bf16[16,2,4096]{2,0,1:T(8,128)(2,1)S(1)} copy(bf16[16,2,4096]{2,1,0:T(2,128)(2,1)} %param.13) | data formatting | bytes 524288 | tf_op args[0]
  8.4 4.5 %collective-permute-start = (bf16[2,16,4096]{2,1,0:T(8,128)(2,1)S(1)}, bf16[2,16,4096]{2,1,0:T(8,128)(2,1)}, u32[]{:S(2)}, u32[]{:S(2)}) collective-permute-start(bf16[2,16,4096]{2,1,0:T(8,128)(2,1)S(1)} %bitcast.19), channel_id=1, source_target_pairs={{0,1},{1,2},{2,3},{3,4},{4,5},{5,6},{6,7},{7,8},{8,9},{9,10},{10,1... | collective-permute-start | bytes 786440 | tf_op jit(solution)/shard_map/ppermute | solution.py:396
  12.9 2.6 %collective-permute-start.1 = (bf16[2,16,4096]{2,1,0:T(8,128)(2,1)S(1)}, bf16[2,16,4096]{2,1,0:T(8,128)(2,1)}, u32[]{:S(2)}, u32[]{:S(2)}) collective-permute-start(bf16[2,16,4096]{2,1,0:T(8,128)(2,1)S(1)} %bitcast.20), channel_id=1, source_target_pairs={{1,0},{2,1},{3,2},{4,3},{5,4},{6,5},{7,6},{8,7},{9,8},{10,9},{11,1... | collective-permute-start | bytes 786440 | tf_op jit(solution)/shard_map/ppermute | solution.py:397
  15.5 0.8 reshape.36
  16.3 0.3 copy.21
  16.6 0.1 mul.46
  16.8 2.5 %multiply_convert_fusion.1 = (bf16[4,256,128]{2,1,0:T(8,128)(2,1)S(1)}, bf16[4,256,128]{2,1,0:T(8,128)(2,1)S(1)}, bf16[4,256,128]{2,1,0:T(8,128)(2,1)S(1)}, bf16[4,256,128]{2,1,0:T(8,128)(2,1)S(1)}) fusion(f32[4,256]{1,0:T(4,128)S(1)} %compare_select_fusion, s32[4,256]{1,0:T(4,128)S(1)} %mul.46), kind=kLoop, calls=%fused_computation.11 | loop fusion | flops 2752512 | bytes 1056768 | tf_op jit(solution)/shard_map/convert.7
  19.3 0.0 copy-start.15
  19.3 0.0 copy-start.13
  19.3 0.0 copy-start.14
  19.3 0.0 copy-start.6
  19.3 0.0 copy-start.7
  19.4 0.0 copy-start.8
  19.4 0.1 maximum_bitcast_fusion
  19.5 0.0 copy-start
  19.5 0.1 pad_maximum_fusion
  19.6 1.5 %dynamic_slice.3.waves_ref = s32[4]{0:T(128)} dynamic-slice(s32[1024]{0:T(1024)} %param.18, s32[]{:T(128)S(6)} %select_n.31), dynamic_slice_sizes={4} | dynamic-slice | bytes 36 | tf_op jit(solution)/shard_map/dynamic_slice | solution.py:442
  21.1 0.0 copy-done.15
  21.1 0.1 broadcast_in_dim_tile.4.gamma_ref
  21.2 0.0 copy-done.13
  21.2 0.7 copy.24
  21.9 0.0 copy-done.14
  21.9 0.7 copy.25
  22.7 0.0 collective-permute-done.prev_ref
  22.7 0.0 collective-permute-done.1.next_ref
  22.7 0.0 copy-done.6
  22.7 0.0 copy-done.7
  22.7 0.0 copy-done.8
  22.7 0.0 copy-start.9
  22.7 0.7 copy-done.9
  23.5 4.3 %interp_fourier.1.sent_ref = bf16[512,128]{1,0:T(8,128)(2,1)S(1)} custom-call(s32[1]{0:T(128)} %bitcast.row_start_ref, bf16[2,16,4096]{2,1,0:T(8,128)(2,1)} %collective-permute-done.prev_ref, bf16[2,16,4096]{2,1,0:T(8,128)(2,1)S(1)} %bitcast.21, bf16[2,16,4096]{2,1,0:T(8,128)(2,1)} %collective-permute-done.1.next_ref, s32[2,4096]{1,0:T(2,128)S(1)} %copy-done.6, ...), custom_call_target="tpu_custom_call" | custom-call | tf_op jit(solution)/shard_map/interp_fourier/pallas_call | solution.py:415
  27.8 0.0 copy-start.4
  27.8 0.6 copy-done.4
  28.4 0.0 copy-done
  28.4 0.0 copy-done.12
  28.4 39.2 %legendre_exchange.1.got_ref = bf16[512,128]{1,0:T(8,128)(2,1)S(1)} custom-call(bf16[512,128]{1,0:T(8,128)(2,1)S(1)} %interp_fourier.1.sent_ref, bf16[4,2,256,512]{3,2,1,0:T(8,128)(2,1)S(1)} %copy-done, f32[32,1]{1,0:T(8,128)S(1)} %broadcast_in_dim_tile.4.gamma_ref, s32[4]{0:T(128)S(1)} %copy-done.12), custom_call_target="tpu_custom_call" | custom-call | tf_op jit(solution)/shard_map/legendre_exchange/pallas_call | solution.py:444
  67.6 0.0 all-gather.2.cloned.1.call-done.optics_ref
  67.6 1.2 %copy-done.1 = bf16[512,1024]{1,0:T(8,128)(2,1)S(1)} copy-done((bf16[512,1024]{1,0:T(8,128)(2,1)S(1)}, bf16[512,1024]{1,0:T(8,128)(2,1)}, u32[]{:S(2)}) %copy-start.1) | copy-done | bytes 1048600
  68.8 0.8 copy-done.2
  69.6 0.8 copy-done.3
  70.5 0.7 copy-done.10
  71.2 0.7 copy-done.11
  71.9 2.6 %radiation.1.heat_ref = bf16[16,1024]{1,0:T(8,128)(2,1)S(1)} custom-call(bf16[2,16,4096]{2,1,0:T(8,128)(2,1)S(1)} %bitcast.22, s32[1,1024]{1,0:T(1,128)S(1)} %copy-done.11, bf16[512,1024]{1,0:T(8,128)(2,1)S(1)} %copy-done.1, f32[128,16]{1,0:T(8,128)S(1)} %bitcast.24, f32[128,16]{1,0:T(8,128)S(1)} %bitcast.25, f32[16,128]{1,0:T(8,128)S(1)} %bitcast.26), custom_call_target="tpu_custom_call" | custom-call | tf_op jit(solution)/shard_map/radiation/pallas_call | solution.py:433
  74.5 0.7 copy-done.5
  75.1 1.1 %inverse_fourier.1 = bf16[2,16,4096]{2,1,0:T(8,128)(2,1)S(1)} custom-call(bf16[512,128]{1,0:T(8,128)(2,1)S(1)} %legendre_exchange.1.got_ref, bf16[2048,256]{1,0:T(8,128)(2,1)S(1)} %bitcast.18, s32[4,256]{1,0:T(4,128)S(1)} %copy-done.5, bf16[16,1024]{1,0:T(8,128)(2,1)S(1)} %radiation.1.heat_ref), custom_call_target="tpu_custom_call" | custom-call | tf_op jit(solution)/shard_map/inverse_fourier/pallas_call | solution.py:466
  76.2 1.0 %copy.26 = bf16[16,2,4096]{2,1,0:T(2,128)(2,1)} copy(bf16[16,2,4096]{2,0,1:T(8,128)(2,1)S(1)} %bitcast.23) | data formatting | bytes 524288 | tf_op jit(solution)/shard_map/transpose | solution.py:475
  (10 shorter events, 0.0 us)
Async XLA Ops:
  6.5 61.0 %all-gather.2.cloned.1.call-start = ((), (), s32[]{:S(2)}) async-start(), calls=%async_computation | async-start | bytes 1081344 | tf_op jit(solution)/shard_map/all_gather | solution.py:398
  8.4 14.3 %collective-permute-start = (bf16[2,16,4096]{2,1,0:T(8,128)(2,1)S(1)}, bf16[2,16,4096]{2,1,0:T(8,128)(2,1)}, u32[]{:S(2)}, u32[]{:S(2)}) collective-permute-start(bf16[2,16,4096]{2,1,0:T(8,128)(2,1)S(1)} %bitcast.19), channel_id=1, source_target_pairs={{0,1},{1,2},{2,3},{3,4},{4,5},{5,6},{6,7},{7,8},{8,9},{9,10},{10,1... | collective-permute-start | bytes 786440 | tf_op jit(solution)/shard_map/ppermute | solution.py:396
  12.9 9.8 %collective-permute-start.1 = (bf16[2,16,4096]{2,1,0:T(8,128)(2,1)S(1)}, bf16[2,16,4096]{2,1,0:T(8,128)(2,1)}, u32[]{:S(2)}, u32[]{:S(2)}) collective-permute-start(bf16[2,16,4096]{2,1,0:T(8,128)(2,1)S(1)} %bitcast.20), channel_id=1, source_target_pairs={{1,0},{2,1},{3,2},{4,3},{5,4},{6,5},{7,6},{8,7},{9,8},{10,9},{11,1... | collective-permute-start | bytes 786440 | tf_op jit(solution)/shard_map/ppermute | solution.py:397
  19.3 1.8 %copy-start.15 = (f32[16]{0:T(128)S(1)}, f32[16]{0:T(128)}, u32[]{:S(2)}) copy-start(f32[16]{0:T(128)} %param.20) | copy-start | bytes 196
  19.3 1.9 %copy-start.13 = (f32[16,128]{1,0:T(8,128)S(1)}, f32[16,128]{1,0:T(8,128)}, u32[]{:S(2)}) copy-start(f32[16,128]{1,0:T(8,128)} %param.23) | copy-start | bytes 24580
  19.3 2.6 %copy-start.14 = (f32[16,128]{1,0:T(8,128)S(1)}, f32[16,128]{1,0:T(8,128)}, u32[]{:S(2)}) copy-start(f32[16,128]{1,0:T(8,128)} %param.24) | copy-start | bytes 24580
  19.3 3.4 %copy-start.6 = (s32[2,4096]{1,0:T(2,128)S(1)}, s32[2,4096]{1,0:T(2,128)}, u32[]{:S(2)}) copy-start(s32[2,4096]{1,0:T(2,128)} %row_ref.1) | copy-start | bytes 98308
  19.3 3.4 %copy-start.7 = (s32[2,4096]{1,0:T(2,128)S(1)}, s32[2,4096]{1,0:T(2,128)}, u32[]{:S(2)}) copy-start(s32[2,4096]{1,0:T(2,128)} %col_ref.1) | copy-start | bytes 98308
  19.4 3.4 %copy-start.8 = (f32[2,4096]{1,0:T(2,128)S(1)}, f32[2,4096]{1,0:T(2,128)}, u32[]{:S(2)}) copy-start(f32[2,4096]{1,0:T(2,128)} %rw_ref.1) | copy-start | bytes 98308
  19.5 8.9 %copy-start = (bf16[4,2,256,512]{3,2,1,0:T(8,128)(2,1)S(1)}, bf16[4,2,256,512]{3,2,1,0:T(8,128)(2,1)}, u32[]{:S(2)}) copy-start(bf16[4,2,256,512]{3,2,1,0:T(8,128)(2,1)} %table_ref.1) | copy-start | bytes 6291460
  22.7 5.7 %copy-start.12 = (s32[4]{0:T(128)S(1)}, s32[4]{0:T(128)}, u32[]{:S(2)}) copy-start(s32[4]{0:T(128)} %dynamic_slice.3.waves_ref) | copy-start | bytes 52
  22.7 0.8 copy-start.9
  27.8 0.6 copy-start.4
  67.6 1.2 %copy-start.1 = (bf16[512,1024]{1,0:T(8,128)(2,1)S(1)}, bf16[512,1024]{1,0:T(8,128)(2,1)}, u32[]{:S(2)}) copy-start(bf16[512,1024]{1,0:T(8,128)(2,1)} %all-gather.2.cloned.1.call-done.optics_ref) | copy-start | bytes 3145732
  68.8 0.8 copy-start.2
  69.6 0.8 copy-start.3
  70.5 0.7 copy-start.10
  71.2 0.7 copy-start.11
  74.5 0.7 copy-start.5
Sparse Core Ops, SparseCore 0:
  9.9 52.1 all-gather.1
where the time goes:
time: 84.6 us; the launch traced here: 84.1 us
  Pallas kernels  47.1 us (56%)
  between operations  13.6 us (16%)
  local copies, waits for them, and re-layouts  12.7 us (15%)
  starting transfers between devices  7.13 us (8%)
  other arithmetic  2.78 us (3%)
    pallas_call x1, Pallas kernels, shards(): pl.pallas_call(functools.partial(middle_kernel, total_waves - 1), out_sha...  39.2 us
    unnamed x35, local copies, waits for them, and re-layouts  8.91 us
    ppermute x1, starting transfers between devices, shards(): before = lax.ppermute(own, ('grp', 'lat'), up)  4.51 us
    pallas_call x1, Pallas kernels, shards(): pl.pallas_call(forward_kernel, out_shape=jax.ShapeDtypeStruct((2 * device...  4.29 us
    ppermute x1, starting transfers between devices, shards(): after = lax.ppermute(own, ('grp', 'lat'), down)  2.62 us
    pallas_call x1, Pallas kernels, shards(): pl.pallas_call(radiation_kernel, out_shape=jax.ShapeDtypeStruct((levels,...  2.58 us
    another operation x1, other arithmetic  2.53 us
  transfers between devices with their start and end apart: 3, of which 0 were waited for; matrix products, arithmetic and copies ran while one was open for 10% of the time, Pallas kernels for 52%

commit v1 on v0

v1 whole, which is shorter than its diff:
```python
import functools
import math

import jax
import jax.numpy as jnp
from jax import lax
from jax.experimental import pallas as pl
from jax.experimental.pallas import tpu as pltpu
from jax.sharding import PartitionSpec as P

F32 = jnp.float32
BF16 = jnp.bfloat16
RADIX = 32
HALF = RADIX // 2 + 1
VMEM_LIMIT = 62 * 1024 * 1024
MESH = pl.DeviceIdType.MESH


def cplx(angle_num, angle_den):
    turn = 2.0 * math.pi * angle_num / angle_den
    return math.cos(turn), math.sin(turn)


def real_fft(planes):
    count = len(planes)
    if count == 2:
        return [(planes[0] + planes[1], None), (planes[0] - planes[1], None)]
    even = real_fft(planes[0::2])
    odd = real_fft(planes[1::2])
    half = count // 2
    out = []
    for k in range(half + 1):

        def pick(spec):
            kk = k % half
            if kk <= half // 2:
                return spec[kk]
            re, im = spec[half - kk]
            return re, (None if im is None else -im)

        er, ei = pick(even)
        orr, oi = pick(odd)
        c, s = cplx(k, count)
        if k == 0:
            out.append((er + orr, None))
        elif k == half:
            out.append((er - orr, None))
        elif 4 * k == count:
            out.append((er, -orr))
        else:
            if oi is None:
                tr, ti = c * orr, -s * orr
            else:
                tr, ti = c * orr + s * oi, c * oi - s * orr
            out.append((er + tr, ti if ei is None else ei + ti))
    return out


def real_ifft(spec):
    half = len(spec) - 1
    count = 2 * half
    if count == 2:
        return [spec[0][0] + spec[1][0], spec[0][0] - spec[1][0]]
    even, odd = [], []
    for k in range(half // 2 + 1):
        xr, xi = spec[k]
        yr, yi = spec[half - k]
        if k == 0:
            even.append((xr + yr, None))
            odd.append((xr - yr, None))
        elif 2 * k == half:
            even.append((xr + xr, None))
            odd.append((-(xi + xi), None))
        else:
            even.append((xr + yr, xi - yi))
            dr, di = xr - yr, xi + yi
            c, s = cplx(k, count)
            odd.append((c * dr - s * di, c * di + s * dr))
    ev, od = real_ifft(even), real_ifft(odd)
    return [plane for pair in zip(ev, od) for plane in pair]


def one_hot(shape, want):
    rows = lax.broadcasted_iota(jnp.int32, shape, 0)
    cols = lax.broadcasted_iota(jnp.int32, shape, 1)
    return jnp.where(want(rows) == cols, 1.0, 0.0).astype(BF16)


def lat_first(row):
    return (row % 32) * 16 + ((row // 32) % 2) * 8 + row // 64


def group_first(row):
    return (row % 8) * 64 + ((row // 8) % 2) * 32 + row // 16


def natural(row):
    return (row // 64) * 64 + (row % 2) * 32 + (row % 64) // 2


def unnatural(row):
    return (row // 64) * 64 + (row % 32) * 2 + (row % 64) // 32


def permuted(matrix, data):
    return jnp.dot(matrix, data, preferred_element_type=F32)


def legendre_step(north_in, south_in, table_ref, gamma, waves_ref, first, turn, trunc):
    to_north, to_south, from_north, from_south = turn
    north = permuted(to_north, north_in)
    south = permuted(to_south, south_in)
    sym = jnp.transpose(north + south).astype(BF16)
    anti = jnp.transpose(north - south).astype(BF16)
    half_degree = table_ref.shape[3]
    steps = lax.broadcasted_iota(jnp.int32, (1, half_degree), 1)
    norm = float(trunc * (trunc + 1))
    even_rows, odd_rows = [], []
    for s in range(4):
        pair = []
        for p, source in enumerate((sym, anti)):
            table = table_ref[s, p]
            spec = jnp.dot(source[32 * s : 32 * s + 32], table, preferred_element_type=F32)
            degree = (waves_ref[first + s] + 2 * steps + p).astype(F32)
            divisor = 1.0 + gamma * (degree * (degree + 1.0)) / norm
            solved = (spec / divisor).astype(BF16)
            pair.append(
                4.0
                * lax.dot_general(
                    solved, table, (((1,), (1,)), ((), ())), preferred_element_type=F32
                )
            )
        even_rows.append(pair[0])
        odd_rows.append(pair[1])
    even = jnp.concatenate(even_rows, axis=0)
    odd = jnp.concatenate(odd_rows, axis=0)
    north = jnp.transpose(even + odd).astype(BF16)
    south = jnp.transpose(even - odd).astype(BF16)
    return permuted(from_north, north).astype(BF16), permuted(from_south, south).astype(BF16)


def interpolate(start, sources, row_ref, col_ref, rw_ref, cw_ref, departed_ref):
    levels, lon = departed_ref.shape[1:]
    sub = lax.broadcasted_iota(jnp.int32, (8, lon), 0) - 2
    lon_ids = lax.broadcasted_iota(jnp.int32, (1, lon), 1)
    for i in range(2):
        rel_row = row_ref[i : i + 1, :] - (start + i)
        rel_col = ((col_ref[i : i + 1, :] - lon_ids + 2) & (lon - 1)) - 2
        a = rw_ref[i : i + 1, :]
        b = cw_ref[i : i + 1, :]
        row_w = jnp.where(rel_row == sub, 1.0 - a, 0.0) + jnp.where(rel_row == sub - 1, a, 0.0)
        col_w = jnp.where(rel_col == sub, 1.0 - b, 0.0) + jnp.where(rel_col == sub - 1, b, 0.0)
        shifted = [
            row_w if dc == 0 else pltpu.roll(row_w, dc % lon, 1) for dc in range(-2, 4)
        ]
        for h in range(levels // 8):
            total = None
            for dc in range(-2, 4):
                mixed = None
                for dr in range(5):
                    term = shifted[dc + 2][dr : dr + 1, :] * sources[i + dr, 8 * h : 8 * h + 8, :]
                    mixed = term if mixed is None else mixed + term
                if dc != 0:
                    mixed = pltpu.roll(mixed, (-dc) % lon, 1)
                term = col_w[dc + 2 : dc + 3, :] * mixed
                total = term if total is None else total + term
            departed_ref[i, 8 * h : 8 * h + 8, :] = total


def forward_waves(departed_ref, z_ref, table_ref, fold, ft_ref, out_ref):
    levels, lon = departed_ref.shape[1:]
    for i in range(2):
        planes = [
            departed_ref[i, :, 128 * j : 128 * j + 128].astype(BF16).astype(F32)
            for j in range(RADIX)
        ]
        for k, (re, im) in enumerate(real_fft(planes)):
            at = 2 * levels * k + levels * i
            z_ref[at : at + levels, 0:128] = re.astype(BF16)
            z_ref[at : at + levels, 128:256] = (
                jnp.zeros((levels, 128), BF16) if im is None else im.astype(BF16)
            )
    scale = math.sqrt(2.0 / lon)
    r = 2 * levels
    for c in range(8):
        prod = lax.dot_general(
            z_ref[...], table_ref[256 * c : 256 * c + 256, :],
            (((1,), (1,)), ((), ())), preferred_element_type=F32,
        )
        got = prod[0:r]
        for k in range(1, HALF):
            got = jnp.where(fold[c // 2] == k, prod[r * k : r * k + r], got)
        got = got * scale
        for i in range(2):
            ft_ref[128 * i + 16 * c : 128 * i + 16 * c + 16, :] = got[16 * i : 16 * i + 16]
    swapped = jnp.transpose(ft_ref[...])
    parts = [swapped[:, 128 * i : 128 * i + 128].reshape(32, 1, 8, 128) for i in range(2)]
    out_ref[...] = jnp.concatenate(parts, axis=1).reshape(512, 128).astype(BF16)


def inverse_waves(got_ref, table_ref, fold, heat, e_ref, out_ref):
    levels, lon = out_ref.shape[1:]
    r = 2 * levels
    rows = got_ref[...].astype(F32).reshape(32, 2, 8, 128)
    turned = [jnp.transpose(rows[:, i].reshape(256, 128)) for i in range(2)]
    for c in range(8):
        piece = jnp.concatenate([t[16 * c : 16 * c + 16] for t in turned], axis=0)
        for k in range(HALF):
            e_ref[r * k : r * k + r, 256 * c : 256 * c + 256] = jnp.where(
                fold[c // 2] == k, piece, 0.0
            ).astype(BF16)
    waves = jnp.dot(e_ref[...], table_ref[...], preferred_element_type=F32)
    scale = 0.5 * math.sqrt(2.0 / lon)
    for i in range(2):
        spec = []
        for k in range(HALF):
            at = r * k + levels * i
            block = waves[at : at + levels]
            re, im = block[:, 0:128], block[:, 128:256]
            if k in (0, HALF - 1):
                spec.append((re + re, None))
            else:
                spec.append((re, im))
        for j, plane in enumerate(real_ifft(spec)):
            warm = heat[:, 128 * j : 128 * j + 128]
            out_ref[i, :, 128 * j : 128 * j + 128] = (plane * scale + warm).astype(BF16)


def coarse_means(own_ref):
    lon = own_ref.shape[2]
    high = lax.broadcasted_iota(jnp.int32, (512, 128), 0)
    low = lax.broadcasted_iota(jnp.int32, (512, 128), 1)
    pool = jnp.where(high // 4 == low, 1.0, 0.0).astype(BF16)
    temps = []
    for b in range(lon // 512):
        part = None
        for e in range(2):
            term = jnp.dot(
                own_ref[e, :, 512 * b : 512 * b + 512], pool, preferred_element_type=F32
            )
            part = term if part is None else part + term
        temps.append(part)
    return (jnp.concatenate(temps, axis=1) * 0.125).astype(BF16).astype(F32)


def radiate(temps, place, optics_ref, kabs, planck, kdown):
    levels, cols = temps.shape
    slot = place & (cols - 1)
    owner = place // cols
    block = (owner & 1) * 16 + owner // 2
    depth_all = None
    for b in range(cols // 256):
        ids = lax.broadcasted_iota(jnp.int32, (256, cols), 0) + 256 * b
        hot = jnp.where(ids == slot, 1.0, 0.0).astype(BF16)
        term = jnp.dot(
            optics_ref[:, 256 * b : 256 * b + 256], hot, preferred_element_type=F32
        )
        depth_all = term if depth_all is None else depth_all + term
    depth = depth_all[0:levels]
    for o in range(1, optics_ref.shape[0] // levels):
        depth = jnp.where(block == o, depth_all[levels * o : levels * o + levels], depth)
    best = lax.Precision.HIGHEST
    emission = 1.0 + jnp.tanh(temps)
    optical = jnp.dot(kabs, depth, precision=best, preferred_element_type=F32)
    source = jnp.dot(planck, emission, precision=best, preferred_element_type=F32)
    return jnp.dot(
        kdown, jnp.exp(-optical) * source, precision=best, preferred_element_type=F32
    ).astype(BF16)


def spread_heat(heat, lon):
    low = lax.broadcasted_iota(jnp.int32, (128, 512), 0)
    high = lax.broadcasted_iota(jnp.int32, (128, 512), 1)
    spread = jnp.where(low == high // 4, 1.0, 0.0).astype(BF16)
    return jnp.concatenate(
        [
            jnp.dot(heat[:, 128 * b : 128 * b + 128], spread, preferred_element_type=F32)
            for b in range(lon // 512)
        ],
        axis=1,
    )


def slot_waves(wave_tile):
    lane = lax.broadcasted_iota(jnp.int32, (128, 1024), 0)
    spot = lax.broadcasted_iota(jnp.int32, (128, 1024), 1)
    pick = jnp.where(lane == 4 * ((spot & 255) // 8) + spot // 256, 1.0, 0.0).astype(BF16)
    high = (wave_tile // 32).astype(F32).astype(BF16)
    low = (wave_tile & 31).astype(F32).astype(BF16)
    spread = 32.0 * jnp.dot(high, pick, preferred_element_type=F32) + jnp.dot(
        low, pick, preferred_element_type=F32
    )
    group = lax.broadcasted_iota(jnp.int32, (8, 1024), 0)
    spot = lax.broadcasted_iota(jnp.int32, (8, 1024), 1)
    flat = jnp.sum(jnp.where(group == (spot & 7), spread, 0.0), axis=0, keepdims=True)
    return [flat[:, 256 * s : 256 * s + 256] for s in range(4)]


def wave_table(rows, table_ref, lon):
    fold = []
    for row in rows:
        kind = row.astype(jnp.int32) & (RADIX - 1)
        fold.append(jnp.minimum(kind, RADIX - kind))
    stacked = jnp.concatenate(rows + [jnp.zeros((124, 256), F32)], axis=0)
    columns = jnp.transpose(stacked)
    step = lax.broadcasted_iota(jnp.int32, (256, 128), 1)
    quarter = lon // 4
    for s in range(4):
        wave = columns[:, s : s + 1].astype(jnp.int32)
        point = (wave * step) & (lon - 1)
        turn = (point + quarter // 2) // quarter
        x = (point - turn * quarter).astype(F32) * (2.0 * math.pi / lon)
        y = x * x
        cosine = 1.0 + y * (-0.5 + y * (1.0 / 24 + y * (-1.0 / 720 + y * (1.0 / 40320))))
        sine = x * (1.0 + y * (-1.0 / 6 + y * (1.0 / 120 + y * (-1.0 / 5040 + y / 362880))))
        swap = (turn & 1) == 1
        c = jnp.where(swap, sine, cosine)
        n = jnp.where(swap, cosine, sine)
        c = jnp.where(((turn + 1) & 2) == 2, -c, c)
        n = jnp.where((turn & 2) == 2, -n, n)
        side = jnp.where((wave & (RADIX - 1)) > RADIX // 2, -1.0, 1.0)
        at = 512 * s
        table_ref[at : at + 256, 0:128] = c.astype(BF16)
        table_ref[at : at + 256, 128:256] = (side * n).astype(BF16)
        table_ref[at + 256 : at + 512, 0:128] = (-n).astype(BF16)
        table_ref[at + 256 : at + 512, 128:256] = (side * c).astype(BF16)
    return fold


def level_column(gamma_ref, rows):
    at = lax.broadcasted_iota(jnp.int32, (rows, 1), 0)
    levels = gamma_ref.shape[0]
    column = jnp.zeros((rows, 1), F32)
    for l in range(levels):
        column = jnp.where(at % levels == l, gamma_ref[l], column)
    return column


def tall(matrix):
    return jnp.transpose(jnp.concatenate([matrix, jnp.zeros((112, 128), F32)], axis=0))[:, 0:16]


def step_kernel(
    trunc, own_ref, row_hbm, col_hbm, rw_hbm, cw_hbm, waves_ref, wave_tile_ref, legendre_hbm,
    gamma_ref, place_hbm, optics_ref, kabs_ref, planck_ref, kdown_ref, out_ref,
    row_ref, col_ref, rw_ref, cw_ref, legendre_ref, place_ref,
    before, after, sources, departed, table, z_ref, ft_ref, e_ref, optics_all,
    sent, got1, send2, got2, send3, got3, send4, got4,
    load_sems, halo_send, halo_recv, opt_send, opt_recv, relay_send, relay_recv,
    send_lat, recv_lat, send_grp, recv_grp, send_grp2, recv_grp2, send_lat2, recv_lat2,
):
    g = lax.axis_index("grp")
    a = lax.axis_index("lat")
    me = g * 32 + a
    levels, lon = own_ref.shape[1:]
    loads = [
        pltpu.make_async_copy(src, dst, load_sems.at[n])
        for n, (src, dst) in enumerate(
            (
                (row_hbm, row_ref), (col_hbm, col_ref), (rw_hbm, rw_ref), (cw_hbm, cw_ref),
                (legendre_hbm, legendre_ref), (place_hbm, place_ref),
            )
        )
    ]
    for load in loads:
        load.start()

    barrier = pltpu.get_barrier_semaphore()
    following = lax.rem(me + 1, 256)
    previous = lax.rem(me + 255, 256)
    for other in (following, previous):
        pl.semaphore_signal(
            barrier, inc=1, device_id=(other // 32, lax.rem(other, 32)), device_id_type=MESH
        )

    @pl.loop(1, 32)
    def _(k):
        pl.semaphore_signal(
            barrier, inc=1, device_id=(g, lax.rem(a + k, 32)), device_id_type=MESH
        )

    @pl.loop(1, 8)
    def _(k):
        pl.semaphore_signal(
            barrier, inc=1, device_id=(lax.rem(g + k, 8), a), device_id_type=MESH
        )

    for i in range(2):
        sources[2 + i] = own_ref[i].astype(F32)
    fold = wave_table(slot_waves(wave_tile_ref[...]), table, lon)

    pl.semaphore_wait(barrier, 40)

    halo = [
        pltpu.make_async_remote_copy(
            src_ref=own_ref, dst_ref=target, send_sem=halo_send.at[n], recv_sem=halo_recv.at[n],
            device_id=(other // 32, lax.rem(other, 32)), device_id_type=MESH,
        )
        for n, (other, target) in enumerate(((following, before), (previous, after)))
    ]
    for move in halo:
        move.start()

    core, chip = lax.rem(a, 2), a // 2

    def optics_rows(which):
        return pl.ds(pl.multiple_of((core * 16 + which) * levels, levels), levels)

    def optics_copy(k, peer, block):
        return pltpu.make_async_remote_copy(
            src_ref=optics_ref, dst_ref=optics_all.at[optics_rows(block)],
            send_sem=opt_send.at[k], recv_sem=opt_recv.at[k],
            device_id=(g, peer * 2 + core), device_id_type=MESH,
        )

    @pl.loop(1, 16)
    def _(k):
        optics_copy(k, lax.rem(chip + k, 16), chip).start()

    optics_all[optics_rows(chip), :] = optics_ref[...]
    temps = coarse_means(own_ref)

    def exchange(source, target, block, send_sems, recv_sems, count, mine, peer_of):
        def copy(k, peer, place):
            return pltpu.make_async_remote_copy(
                src_ref=source.at[pl.ds(pl.multiple_of(peer * block, block), block)],
                dst_ref=target.at[pl.ds(pl.multiple_of(place * block, block), block)],
                send_sem=send_sems.at[k], recv_sem=recv_sems.at[k],
                device_id=peer_of(peer), device_id_type=MESH,
            )

        @pl.loop(1, count)
        def _(k):
            copy(k, lax.rem(mine + k, count), mine).start()

        here = pl.ds(pl.multiple_of(mine * block, block), block)
        target[here, :] = source[here, :]

        def finish():
            @pl.loop(1, count)
            def _(k):
                peer = lax.rem(mine + count - k, count)
                copy(k, lax.rem(mine + k, count), mine).wait_send()
                copy(k, peer, peer).wait_recv()

        return finish

    def over_lat(peer):
        return (g, peer)

    def over_grp(peer):
        return (peer, a)

    for load in loads[:4]:
        load.wait()
    for move in halo:
        move.wait_send()
        move.wait_recv()
    for i in range(2):
        sources[i] = before[i].astype(F32)
        sources[4 + i] = after[i].astype(F32)
    interpolate(2 * me, sources, row_ref, col_ref, rw_ref, cw_ref, departed)
    forward_waves(departed, z_ref, table, fold, ft_ref, sent)

    done = exchange(sent, got1, 16, send_lat, recv_lat, 32, a, over_lat)
    to_group = one_hot((512, 512), lat_first)

    @pl.loop(1, 16)
    def _(k):
        optics_copy(k, lax.rem(chip + k, 16), chip).wait_send()
        optics_copy(k, chip, lax.rem(chip + 16 - k, 16)).wait_recv()

    def relay_copy(which):
        half = optics_all.at[pl.ds(pl.multiple_of(which * (16 * levels), 16 * levels), 16 * levels)]
        return pltpu.make_async_remote_copy(
            src_ref=half, dst_ref=half, send_sem=relay_send.at[0], recv_sem=relay_recv.at[0],
            device_id=(g, chip * 2 + 1 - core), device_id_type=MESH,
        )

    relay_copy(core).start()
    done()
    send2[...] = permuted(to_group, got1[...]).astype(BF16)
    done = exchange(send2, got2, 64, send_grp, recv_grp, 8, g, over_grp)
    turn = (
        one_hot((256, 256), natural),
        one_hot((256, 256), lambda row: natural(255 - row)),
        one_hot((256, 256), unnatural),
        one_hot((256, 256), lambda row: 255 - unnatural(row)),
    )
    gamma = level_column(gamma_ref, 2 * levels)
    loads[4].wait()
    done()
    north, south = legendre_step(
        got2[0:256, :], got2[256:512, :], legendre_ref, gamma, waves_ref, me * 4, turn, trunc
    )
    send3[0:256, :] = north
    send3[256:512, :] = south
    done = exchange(send3, got3, 64, send_grp2, recv_grp2, 8, g, over_grp)
    to_lat = one_hot((512, 512), group_first)
    loads[5].wait()
    relay_copy(core).wait_send()
    relay_copy(1 - core).wait_recv()
    heat = radiate(
        temps, place_ref[...], optics_all, tall(kabs_ref[...]), tall(planck_ref[...]),
        kdown_ref[...],
    )
    done()
    send4[...] = permuted(to_lat, got3[...]).astype(BF16)
    done = exchange(send4, got4, 16, send_lat2, recv_lat2, 32, a, over_lat)
    heat = spread_heat(heat, lon)
    done()
    inverse_waves(got4, table, fold, heat, e_ref, out_ref)


def shards(
    state, dep_row, dep_col, row_weight, col_weight, wave_of, legendre, gamma,
    rad_place, optics, kabs, planck_weight, kdown,
):
    levels, lat_rows, lon = state.shape
    owners = lax.axis_size("lat")
    groups = lax.axis_size("grp")
    trunc = wave_of.shape[0] - 1
    coarse = lon // 4
    rows = 2 * groups * owners
    own = jnp.transpose(state, (1, 0, 2))
    in_vmem = pl.BlockSpec(memory_space=pltpu.VMEM)
    in_smem = pl.BlockSpec(memory_space=pltpu.SMEM)
    in_hbm = pl.BlockSpec(memory_space=pl.ANY)
    dma = pltpu.SemaphoreType.DMA
    result = pl.pallas_call(
        functools.partial(step_kernel, trunc),
        out_shape=jax.ShapeDtypeStruct((lat_rows, levels, lon), BF16),
        in_specs=[
            in_vmem, in_hbm, in_hbm, in_hbm, in_hbm, in_smem, in_vmem, in_hbm,
            in_smem, in_hbm, in_vmem, in_vmem, in_vmem, in_vmem,
        ],
        out_specs=in_vmem,
        scratch_shapes=[
            pltpu.VMEM((lat_rows, lon), jnp.int32),
            pltpu.VMEM((lat_rows, lon), jnp.int32),
            pltpu.VMEM((lat_rows, lon), F32),
            pltpu.VMEM((lat_rows, lon), F32),
            pltpu.VMEM(legendre.shape, BF16),
            pltpu.VMEM((1, coarse), jnp.int32),
            pltpu.VMEM((lat_rows, levels, lon), BF16),
            pltpu.VMEM((lat_rows, levels, lon), BF16),
            pltpu.VMEM((6, levels, lon), F32),
            pltpu.VMEM((2, levels, lon), F32),
            pltpu.VMEM((2048, 256), BF16),
            pltpu.VMEM((HALF * 2 * levels, 256), BF16),
            pltpu.VMEM((256, 256), F32),
            pltpu.VMEM((HALF * 2 * levels, 2048), BF16),
            pltpu.VMEM((owners * levels, coarse), BF16),
        ]
        + [pltpu.VMEM((rows, 128), BF16)] * 8
        + [dma((6,)), dma((2,)), dma((2,)), dma((16,)), dma((16,)), dma((1,)), dma((1,))]
        + [dma((32,)), dma((32,)), dma((8,)), dma((8,))]
        + [dma((8,)), dma((8,)), dma((32,)), dma((32,))],
        compiler_params=pltpu.CompilerParams(
            vmem_limit_bytes=VMEM_LIMIT, collective_id=0, has_side_effects=True
        ),
        name="model_step",
    )(
        own, dep_row, dep_col, row_weight, col_weight, wave_of,
        wave_of.reshape(groups, owners * 4), legendre, gamma, rad_place,
        jnp.transpose(optics), kabs, planck_weight, jnp.transpose(kdown),
    )
    return jnp.transpose(result, (1, 0, 2))


def solution(mesh):
    return jax.shard_map(
        shards,
        mesh=mesh,
        in_specs=(
            P(None, ("grp", "lat"), None),
            P(("grp", "lat"), None),
            P(("grp", "lat"), None),
            P(("grp", "lat"), None),
            P(("grp", "lat"), None),
            P(),
            P(("grp", "lat"), None, None, None),
            P(),
            P(("grp", "lat"), None),
            P(("grp", "lat"), None),
            P(),
            P(),
            P(),
        ),
        out_specs=P(None, ("grp", "lat"), None),
        check_vma=False,
    )
```

time: 84.6 us -> 55.5 us (0.66)
  between operations: 13.6 us -> 0.01 us
  local copies, waits for them, and re-layouts: 12.7 us -> 3.73 us
  starting transfers between devices: 7.13 us -> 0 us
  Pallas kernels: 47.1 us -> 51.6 us
  other arithmetic: 2.78 us -> 0 us
    ppermute x2 -> x0, starting transfers between devices: 7.13 us -> none  [the longest x1 4.51 us: shards(): before = lax.ppermute(own, ('grp', 'lat'), up)]
    unnamed x35 -> x1, local copies, waits for them, and re-layouts: 8.91 us -> 1.8 us
    pallas_call x4 -> x1, Pallas kernels: 47.1 us -> 51.6 us  [shards(): pl.pallas_call(functools.partial(step_kernel, trunc), out_shape=jax.Shape...]
    another operation x3 -> x0, other arithmetic: 2.76 us -> none
    dynamic_slice x1 -> x0, local copies, waits for them, and re-layouts: 1.47 us -> none  [shards(): my_waves = lax.dynamic_slice_in_dim(wave_of, dev_index * 4, 4)]
    transpose x1, local copies, waits for them, and re-layouts: 0.98 us -> 1.93 us  [shards(): return jnp.transpose(result, (1, 0, 2))]
  transfers between devices with their start and end apart: 3 -> 0, of which waited for: 0 -> 0; matrix products, arithmetic and copies ran while one was open for 10% -> 0% of each run, Pallas kernels for 52% -> 0%
where the time goes in v1:
time: 55.5 us; the launch traced here: 55.3 us
  Pallas kernels  51.6 us (93%)
  local copies, waits for them, and re-layouts  3.73 us (7%)
    pallas_call x1, Pallas kernels, shards(): pl.pallas_call(functools.partial(step_kernel, trunc), out_shape=jax.Shape...  51.6 us
    transpose x1, local copies, waits for them, and re-layouts, shards(): return jnp.transpose(result, (1, 0, 2))  1.93 us
    unnamed x1, local copies, waits for them, and re-layouts  1.8 us

profile of v1, /device:TPU:1, one launch (start us, length us, event | category | flops | bytes accessed | tf_op | source)
XLA Modules:
  0.0 55.3 jit_solution(17656610978301984574)
XLA Ops:
  0.0 1.8 %copy.17 = bf16[16,2,4096]{2,0,1:T(8,128)(2,1)} copy(bf16[16,2,4096]{2,1,0:T(2,128)(2,1)} %param.13) | data formatting | bytes 524288 | tf_op args[0]
  1.8 51.6 %model_step.1 = bf16[2,16,4096]{2,1,0:T(8,128)(2,1)} custom-call(bf16[2,16,4096]{2,1,0:T(8,128)(2,1)} %bitcast.8, s32[2,4096]{1,0:T(2,128)} %row_hbm.1, s32[2,4096]{1,0:T(2,128)} %col_hbm.1, f32[2,4096]{1,0:T(2,128)} %rw_hbm.1, f32[2,4096]{1,0:T(2,128)} %cw_hbm.1, s32[1024]{0:T(1024)} %waves_ref.1, s32[8,128]{1,0:T(8,128)} %bitcast.10, ...), custom_call_target="tpu_custom_call" | custom-call | tf_op jit(solution)/shard_map/model_step/pallas_call | solution.py:530
  53.4 1.9 %copy.15 = bf16[16,2,4096]{2,1,0:T(2,128)(2,1)} copy(bf16[16,2,4096]{2,0,1:T(8,128)(2,1)} %bitcast.7) | data formatting | bytes 524288 | tf_op jit(solution)/shard_map/transpose | solution.py:568

commit v2 on v1

--- a/solution.py
+++ b/solution.py
@@ -14,6 +14,7 @@
 HALF = RADIX // 2 + 1
 VMEM_LIMIT = 62 * 1024 * 1024
 MESH = pl.DeviceIdType.MESH
+LAT_STEPS = [8 * y + 2 * x + c for y in (2, 1, 3, 0) for x in (2, 1, 3, 0) for c in (1, 0)]
 
 
 def cplx(angle_num, angle_den):
@@ -86,30 +87,13 @@
     return jnp.where(want(rows) == cols, 1.0, 0.0).astype(BF16)
 
 
-def lat_first(row):
-    return (row % 32) * 16 + ((row // 32) % 2) * 8 + row // 64
-
-
-def group_first(row):
-    return (row % 8) * 64 + ((row // 8) % 2) * 32 + row // 16
-
-
-def natural(row):
-    return (row // 64) * 64 + (row % 2) * 32 + (row % 64) // 2
-
-
-def unnatural(row):
-    return (row // 64) * 64 + (row % 32) * 2 + (row % 64) // 32
-
-
 def permuted(matrix, data):
     return jnp.dot(matrix, data, preferred_element_type=F32)
 
 
 def legendre_step(north_in, south_in, table_ref, gamma, waves_ref, first, turn, trunc):
-    to_north, to_south, from_north, from_south = turn
-    north = permuted(to_north, north_in)
-    south = permuted(to_south, south_in)
+    north = north_in.astype(F32)
+    south = permuted(turn, south_in)
     sym = jnp.transpose(north + south).astype(BF16)
     anti = jnp.transpose(north - south).astype(BF16)
     half_degree = table_ref.shape[3]
@@ -136,7 +120,7 @@
     odd = jnp.concatenate(odd_rows, axis=0)
     north = jnp.transpose(even + odd).astype(BF16)
     south = jnp.transpose(even - odd).astype(BF16)
-    return permuted(from_north, north).astype(BF16), permuted(from_south, south).astype(BF16)
+    return north, permuted(turn, south).astype(BF16)
 
 
 def interpolate(start, sources, row_ref, col_ref, rw_ref, cw_ref, departed_ref):
@@ -167,7 +151,7 @@
             departed_ref[i, 8 * h : 8 * h + 8, :] = total
 
 
-def forward_waves(departed_ref, z_ref, table_ref, fold, ft_ref, out_ref):
+def forward_waves(departed_ref, z_ref, tall_ref, fold, ft_ref, mix_ref, out_ref):
     levels, lon = departed_ref.shape[1:]
     for i in range(2):
         planes = [
@@ -183,10 +167,7 @@
     scale = math.sqrt(2.0 / lon)
     r = 2 * levels
     for c in range(8):
-        prod = lax.dot_general(
-            z_ref[...], table_ref[256 * c : 256 * c + 256, :],
-            (((1,), (1,)), ((), ())), preferred_element_type=F32,
-        )
+        prod = jnp.dot(z_ref[...], tall_ref[c], preferred_element_type=F32)
         got = prod[0:r]
         for k in range(1, HALF):
             got = jnp.where(fold[c // 2] == k, prod[r * k : r * k + r], got)
@@ -194,15 +175,16 @@
         for i in range(2):
             ft_ref[128 * i + 16 * c : 128 * i + 16 * c + 16, :] = got[16 * i : 16 * i + 16]
     swapped = jnp.transpose(ft_ref[...])
-    parts = [swapped[:, 128 * i : 128 * i + 128].reshape(32, 1, 8, 128) for i in range(2)]
-    out_ref[...] = jnp.concatenate(parts, axis=1).reshape(512, 128).astype(BF16)
-
-
-def inverse_waves(got_ref, table_ref, fold, heat, e_ref, out_ref):
+    for i in range(2):
+        mix_ref[pl.ds(i, 256, stride=2), :] = swapped[:, 128 * i : 128 * i + 128]
+    out_ref[...] = mix_ref[...].astype(BF16).reshape(256, 2, 128)
+
+
+def inverse_waves(got_ref, table_ref, fold, heat, e_ref, mix_ref, out_ref):
     levels, lon = out_ref.shape[1:]
     r = 2 * levels
-    rows = got_ref[...].astype(F32).reshape(32, 2, 8, 128)
-    turned = [jnp.transpose(rows[:, i].reshape(256, 128)) for i in range(2)]
+    mix_ref[...] = got_ref[...].reshape(512, 128).astype(F32)
+    turned = [jnp.transpose(mix_ref[pl.ds(i, 256, stride=2), :]) for i in range(2)]
     for c in range(8):
         piece = jnp.concatenate([t[16 * c : 16 * c + 16] for t in turned], axis=0)
         for k in range(HALF):
@@ -284,7 +266,7 @@
 def slot_waves(wave_tile):
     lane = lax.broadcasted_iota(jnp.int32, (128, 1024), 0)
     spot = lax.broadcasted_iota(jnp.int32, (128, 1024), 1)
-    pick = jnp.where(lane == 4 * ((spot & 255) // 8) + spot // 256, 1.0, 0.0).astype(BF16)
+    pick = jnp.where(lane == 4 * (spot & 31) + spot // 256, 1.0, 0.0).astype(BF16)
     high = (wave_tile // 32).astype(F32).astype(BF16)
     low = (wave_tile & 31).astype(F32).astype(BF16)
     spread = 32.0 * jnp.dot(high, pick, preferred_element_type=F32) + jnp.dot(
@@ -292,39 +274,55 @@
     )
     group = lax.broadcasted_iota(jnp.int32, (8, 1024), 0)
     spot = lax.broadcasted_iota(jnp.int32, (8, 1024), 1)
-    flat = jnp.sum(jnp.where(group == (spot & 7), spread, 0.0), axis=0, keepdims=True)
+    flat = jnp.sum(jnp.where(group == (spot & 255) // 32, spread, 0.0), axis=0, keepdims=True)
     return [flat[:, 256 * s : 256 * s + 256] for s in range(4)]
 
 
-def wave_table(rows, table_ref, lon):
+def turn_values(wave, step, lon):
+    quarter = lon // 4
+    point = (wave * step) & (lon - 1)
+    turn = (point + quarter // 2) // quarter
+    x = (point - turn * quarter).astype(F32) * (2.0 * math.pi / lon)
+    y = x * x
+    cosine = 1.0 + y * (-0.5 + y * (1.0 / 24 + y * (-1.0 / 720 + y * (1.0 / 40320))))
+    sine = x * (1.0 + y * (-1.0 / 6 + y * (1.0 / 120 + y * (-1.0 / 5040 + y / 362880))))
+    swap = (turn & 1) == 1
+    c = jnp.where(swap, sine, cosine)
+    n = jnp.where(swap, cosine, sine)
+    c = jnp.where(((turn + 1) & 2) == 2, -c, c)
+    n = jnp.where((turn & 2) == 2, -n, n)
+    side = jnp.where((wave & (RADIX - 1)) > RADIX // 2, -1.0, 1.0)
+    return c.astype(BF16), (side * n).astype(BF16), (-n).astype(BF16), (side * c).astype(BF16)
+
+
+def fold_of(rows):
     fold = []
     for row in rows:
         kind = row.astype(jnp.int32) & (RADIX - 1)
         fold.append(jnp.minimum(kind, RADIX - kind))
-    stacked = jnp.concatenate(rows + [jnp.zeros((124, 256), F32)], axis=0)
-    columns = jnp.transpose(stacked)
+    return fold
+
+
+def tall_table(rows, tall_ref, lon):
+    step = lax.broadcasted_iota(jnp.int32, (128, 256), 0)
+    for s in range(4):
+        a, b, c, d = turn_values(rows[s].astype(jnp.int32), step, lon)
+        tall_ref[2 * s, 0:128, :] = a
+        tall_ref[2 * s, 128:256, :] = b
+        tall_ref[2 * s + 1, 0:128, :] = c
+        tall_ref[2 * s + 1, 128:256, :] = d
+
+
+def wide_table(rows, table_ref, lon):
+    columns = jnp.transpose(jnp.concatenate(rows + [jnp.zeros((124, 256), F32)], axis=0))
     step = lax.broadcasted_iota(jnp.int32, (256, 128), 1)
-    quarter = lon // 4
     for s in range(4):
-        wave = columns[:, s : s + 1].astype(jnp.int32)
-        point = (wave * step) & (lon - 1)
-        turn = (point + quarter // 2) // quarter
-        x = (point - turn * quarter).astype(F32) * (2.0 * math.pi / lon)
-        y = x * x
-        cosine = 1.0 + y * (-0.5 + y * (1.0 / 24 + y * (-1.0 / 720 + y * (1.0 / 40320))))
-        sine = x * (1.0 + y * (-1.0 / 6 + y * (1.0 / 120 + y * (-1.0 / 5040 + y / 362880))))
-        swap = (turn & 1) == 1
-        c = jnp.where(swap, sine, cosine)
-        n = jnp.where(swap, cosine, sine)
-        c = jnp.where(((turn + 1) & 2) == 2, -c, c)
-        n = jnp.where((turn & 2) == 2, -n, n)
-        side = jnp.where((wave & (RADIX - 1)) > RADIX // 2, -1.0, 1.0)
+        a, b, c, d = turn_values(columns[:, s : s + 1].astype(jnp.int32), step, lon)
         at = 512 * s
-        table_ref[at : at + 256, 0:128] = c.astype(BF16)
-        table_ref[at : at + 256, 128:256] = (side * n).astype(BF16)
-        table_ref[at + 256 : at + 512, 0:128] = (-n).astype(BF16)
-        table_ref[at + 256 : at + 512, 128:256] = (side * c).astype(BF16)
-    return fold
+        table_ref[at : at + 256, 0:128] = a
+        table_ref[at : at + 256, 128:256] = b
+        table_ref[at + 256 : at + 512, 0:128] = c
+        table_ref[at + 256 : at + 512, 128:256] = d
 
 
 def level_column(gamma_ref, rows):
@@ -341,26 +339,27 @@
 
 
 def step_kernel(
-    trunc, own_ref, row_hbm, col_hbm, rw_hbm, cw_hbm, waves_ref, wave_tile_ref, legendre_hbm,
-    gamma_ref, place_hbm, optics_ref, kabs_ref, planck_ref, kdown_ref, out_ref,
-    row_ref, col_ref, rw_ref, cw_ref, legendre_ref, place_ref,
-    before, after, sources, departed, table, z_ref, ft_ref, e_ref, optics_all,
-    sent, got1, send2, got2, send3, got3, send4, got4,
+    trunc, own_ref, row_hbm, col_hbm, rw_hbm, cw_hbm, waves_ref, wave_tile_hbm, legendre_hbm,
+    gamma_ref, place_hbm, optics_hbm, kabs_hbm, planck_hbm, kdown_hbm, out_ref,
+    row_ref, col_ref, rw_ref, cw_ref, wave_tile_ref, legendre_ref, place_ref, optics_ref,
+    kabs_ref, planck_ref, kdown_ref,
+    before, after, sources, departed, table, tall_ref, z_ref, ft_ref, mix_ref, e_ref, optics_all,
+    sent, got, answer, back,
     load_sems, halo_send, halo_recv, opt_send, opt_recv, relay_send, relay_recv,
-    send_lat, recv_lat, send_grp, recv_grp, send_grp2, recv_grp2, send_lat2, recv_lat2,
+    out_send, out_recv, back_send, back_recv, ready,
 ):
     g = lax.axis_index("grp")
     a = lax.axis_index("lat")
     me = g * 32 + a
     levels, lon = own_ref.shape[1:]
+    moves = (
+        (wave_tile_hbm, wave_tile_ref), (optics_hbm, optics_ref),
+        (row_hbm, row_ref), (col_hbm, col_ref), (rw_hbm, rw_ref), (cw_hbm, cw_ref),
+        (legendre_hbm, legendre_ref), (place_hbm, place_ref), (kabs_hbm, kabs_ref),
+        (planck_hbm, planck_ref), (kdown_hbm, kdown_ref),
+    )
     loads = [
-        pltpu.make_async_copy(src, dst, load_sems.at[n])
-        for n, (src, dst) in enumerate(
-            (
-                (row_hbm, row_ref), (col_hbm, col_ref), (rw_hbm, rw_ref), (cw_hbm, cw_ref),
-                (legendre_hbm, legendre_ref), (place_hbm, place_ref),
-            )
-        )
+        pltpu.make_async_copy(src, dst, load_sems.at[n]) for n, (src, dst) in enumerate(moves)
     ]
     for load in loads:
         load.start()
@@ -387,7 +386,11 @@
 
     for i in range(2):
         sources[2 + i] = own_ref[i].astype(F32)
-    fold = wave_table(slot_waves(wave_tile_ref[...]), table, lon)
+    loads[0].wait()
+    rows = slot_waves(wave_tile_ref[...])
+    fold = fold_of(rows)
+    tall_table(rows, tall_ref, lon)
+    loads[1].wait()
 
     pl.semaphore_wait(barrier, 40)
 
@@ -400,6 +403,12 @@
     ]
     for move in halo:
         move.start()
+
+    @pl.loop(1, 8)
+    def _(k):
+        pl.semaphore_signal(
+            ready, inc=1, device_id=(lax.rem(g + k, 8), a), device_id_type=MESH
+        )
 
     core, chip = lax.rem(a, 2), a // 2
 
@@ -419,51 +428,43 @@
 
     optics_all[optics_rows(chip), :] = optics_ref[...]
     temps = coarse_means(own_ref)
-
-    def exchange(source, target, block, send_sems, recv_sems, count, mine, peer_of):
-        def copy(k, peer, place):
-            return pltpu.make_async_remote_copy(
-                src_ref=source.at[pl.ds(pl.multiple_of(peer * block, block), block)],
-                dst_ref=target.at[pl.ds(pl.multiple_of(place * block, block), block)],
-                send_sem=send_sems.at[k], recv_sem=recv_sems.at[k],
-                device_id=peer_of(peer), device_id_type=MESH,
-            )
-
-        @pl.loop(1, count)
+    wide_table(rows, table, lon)
+
+    def exchange(source, target, send_sem, recv_sem):
+        def send(z, lat):
+            pltpu.make_async_remote_copy(
+                src_ref=source.at[z * 32 + lat], dst_ref=target.at[me],
+                send_sem=send_sem.at[0], recv_sem=recv_sem.at[0],
+                device_id=(z, lat), device_id_type=MESH,
+            ).start()
+
+        @pl.loop(0, 7)
         def _(k):
-            copy(k, lax.rem(mine + k, count), mine).start()
-
-        here = pl.ds(pl.multiple_of(mine * block, block), block)
-        target[here, :] = source[here, :]
-
-        def finish():
-            @pl.loop(1, count)
-            def _(k):
-                peer = lax.rem(mine + count - k, count)
-                copy(k, lax.rem(mine + k, count), mine).wait_send()
-                copy(k, peer, peer).wait_recv()
-
-        return finish
-
-    def over_lat(peer):
-        return (g, peer)
-
-    def over_grp(peer):
-        return (peer, a)
-
-    for load in loads[:4]:
+            z = g ^ jnp.where(k < 4, 4 + k, 7 - k)
+            for step in LAT_STEPS:
+                send(z, a ^ step)
+
+        for step in LAT_STEPS[:-1]:
+            send(g, a ^ step)
+        target[me] = source[me]
+        return pltpu.make_async_remote_copy(
+            src_ref=source.at[pl.ds(0, 255)], dst_ref=target.at[pl.ds(0, 255)],
+            send_sem=send_sem.at[0], recv_sem=recv_sem.at[0],
+            device_id=(lax.rem(g + 1, 8), a), device_id_type=MESH,
+        )
+
+    for load in loads[2:6]:
         load.wait()
     for move in halo:
-        move.wait_send()
         move.wait_recv()
     for i in range(2):
         sources[i] = before[i].astype(F32)
         sources[4 + i] = after[i].astype(F32)
     interpolate(2 * me, sources, row_ref, col_ref, rw_ref, cw_ref, departed)
-    forward_waves(departed, z_ref, table, fold, ft_ref, sent)
-
-    done = exchange(sent, got1, 16, send_lat, recv_lat, 32, a, over_lat)
-    to_group = one_hot((512, 512), lat_first)
+    forward_waves(departed, z_ref, tall_ref, fold, ft_ref, mix_ref, sent)
+    pl.semaphore_wait(ready, 7)
+
+    outward = exchange(sent, got, out_send, out_recv)
 
     @pl.loop(1, 16)
     def _(k):
@@ -478,38 +479,31 @@
         )
 
     relay_copy(core).start()
-    done()
-    send2[...] = permuted(to_group, got1[...]).astype(BF16)
-    done = exchange(send2, got2, 64, send_grp, recv_grp, 8, g, over_grp)
-    turn = (
-        one_hot((256, 256), natural),
-        one_hot((256, 256), lambda row: natural(255 - row)),
-        one_hot((256, 256), unnatural),
-        one_hot((256, 256), lambda row: 255 - unnatural(row)),
-    )
+    turn = one_hot((256, 256), lambda row: 255 - row)
     gamma = level_column(gamma_ref, 2 * levels)
-    loads[4].wait()
-    done()
-    north, south = legendre_step(
-        got2[0:256, :], got2[256:512, :], legendre_ref, gamma, waves_ref, me * 4, turn, trunc
-    )
-    send3[0:256, :] = north
-    send3[256:512, :] = south
-    done = exchange(send3, got3, 64, send_grp2, recv_grp2, 8, g, over_grp)
-    to_lat = one_hot((512, 512), group_first)
-    loads[5].wait()
-    relay_copy(core).wait_send()
+    for load in loads[6:]:
+        load.wait()
     relay_copy(1 - core).wait_recv()
     heat = radiate(
         temps, place_ref[...], optics_all, tall(kabs_ref[...]), tall(planck_ref[...]),
         kdown_ref[...],
     )
-    done()
-    send4[...] = permuted(to_lat, got3[...]).astype(BF16)
-    done = exchange(send4, got4, 16, send_lat2, recv_lat2, 32, a, over_lat)
+    outward.wait_recv()
+    north, south = legendre_step(
+        got[0:128].reshape(256, 128), got[128:256].reshape(256, 128), legendre_ref, gamma,
+        waves_ref, me * 4, turn, trunc,
+    )
+    answer[0:128] = north.reshape(128, 2, 128)
+    answer[128:256] = south.reshape(128, 2, 128)
+    homeward = exchange(answer, back, back_send, back_recv)
     heat = spread_heat(heat, lon)
-    done()
-    inverse_waves(got4, table, fold, heat, e_ref, out_ref)
+    homeward.wait_recv()
+    inverse_waves(back, table, fold, heat, e_ref, mix_ref, out_ref)
+    for move in halo:
+        move.wait_send()
+    relay_copy(core).wait_send()
+    outward.wait_send()
+    homeward.wait_send()
 
 
 def shards(
@@ -521,18 +515,17 @@
     groups = lax.axis_size("grp")
     trunc = wave_of.shape[0] - 1
     coarse = lon // 4
-    rows = 2 * groups * owners
     own = jnp.transpose(state, (1, 0, 2))
     in_vmem = pl.BlockSpec(memory_space=pltpu.VMEM)
     in_smem = pl.BlockSpec(memory_space=pltpu.SMEM)
-    in_hbm = pl.BlockSpec(memory_space=pl.ANY)
+    in_hbm = pl.BlockSpec(memory_space=pltpu.HBM)
     dma = pltpu.SemaphoreType.DMA
     result = pl.pallas_call(
         functools.partial(step_kernel, trunc),
         out_shape=jax.ShapeDtypeStruct((lat_rows, levels, lon), BF16),
         in_specs=[
-            in_vmem, in_hbm, in_hbm, in_hbm, in_hbm, in_smem, in_vmem, in_hbm,
-            in_smem, in_hbm, in_vmem, in_vmem, in_vmem, in_vmem,
+            in_vmem, in_hbm, in_hbm, in_hbm, in_hbm, in_smem, in_hbm, in_hbm,
+            in_smem, in_hbm, in_hbm, in_hbm, in_hbm, in_hbm,
         ],
         out_specs=in_vmem,
         scratch_shapes=[
@@ -540,22 +533,29 @@
             pltpu.VMEM((lat_rows, lon), jnp.int32),
             pltpu.VMEM((lat_rows, lon), F32),
             pltpu.VMEM((lat_rows, lon), F32),
+            pltpu.VMEM((groups, owners * 4), jnp.int32),
             pltpu.VMEM(legendre.shape, BF16),
             pltpu.VMEM((1, coarse), jnp.int32),
+            pltpu.VMEM((levels, coarse), BF16),
+            pltpu.VMEM((levels, 128), F32),
+            pltpu.VMEM((levels, 128), F32),
+            pltpu.VMEM((levels, 128), F32),
             pltpu.VMEM((lat_rows, levels, lon), BF16),
             pltpu.VMEM((lat_rows, levels, lon), BF16),
             pltpu.VMEM((6, levels, lon), F32),
             pltpu.VMEM((2, levels, lon), F32),
             pltpu.VMEM((2048, 256), BF16),
+            pltpu.VMEM((8, 256, 256), BF16),
             pltpu.VMEM((HALF * 2 * levels, 256), BF16),
             pltpu.VMEM((256, 256), F32),
+            pltpu.VMEM((512, 128), F32),
             pltpu.VMEM((HALF * 2 * levels, 2048), BF16),
             pltpu.VMEM((owners * levels, coarse), BF16),
         ]
-        + [pltpu.VMEM((rows, 128), BF16)] * 8
-        + [dma((6,)), dma((2,)), dma((2,)), dma((16,)), dma((16,)), dma((1,)), dma((1,))]
-        + [dma((32,)), dma((32,)), dma((8,)), dma((8,))]
-        + [dma((8,)), dma((8,)), dma((32,)), dma((32,))],
+        + [pltpu.VMEM((groups * owners, 2, 128), BF16)] * 4
+        + [dma((11,)), dma((2,)), dma((2,)), dma((16,)), dma((16,)), dma((1,)), dma((1,))]
+        + [dma((1,))] * 4
+        + [pltpu.SemaphoreType.REGULAR],
         compiler_params=pltpu.CompilerParams(
             vmem_limit_bytes=VMEM_LIMIT, collective_id=0, has_side_effects=True
         ),

time: 55.5 us -> 47 us (0.85)
  Pallas kernels: 51.6 us -> 43.1 us
    pallas_call x1, Pallas kernels: 51.6 us -> 43.1 us  [shards(): pl.pallas_call(functools.partial(step_kernel, trunc), out_shape=jax.Shape...]
where the time goes in v2:
time: 47 us; the launch traced here: 46.8 us
  Pallas kernels  43.1 us (92%)
  local copies, waits for them, and re-layouts  3.73 us (8%)
    pallas_call x1, Pallas kernels, shards(): pl.pallas_call(functools.partial(step_kernel, trunc), out_shape=jax.Shape...  43.1 us
    transpose x1, local copies, waits for them, and re-layouts, shards(): return jnp.transpose(result, (1, 0, 2))  1.93 us
    unnamed x1, local copies, waits for them, and re-layouts  1.8 us

profile of v2, /device:TPU:1, one launch (start us, length us, event | category | flops | bytes accessed | tf_op | source)
XLA Modules:
  0.0 46.8 jit_solution(15044653214272620180)
XLA Ops:
  0.0 1.8 %copy.17 = bf16[16,2,4096]{2,0,1:T(8,128)(2,1)} copy(bf16[16,2,4096]{2,1,0:T(2,128)(2,1)} %param.13) | data formatting | bytes 524288 | tf_op args[0]
  1.8 43.1 %model_step.1 = bf16[2,16,4096]{2,1,0:T(8,128)(2,1)} custom-call(bf16[2,16,4096]{2,1,0:T(8,128)(2,1)} %bitcast.8, s32[2,4096]{1,0:T(2,128)} %row_hbm.1, s32[2,4096]{1,0:T(2,128)} %col_hbm.1, f32[2,4096]{1,0:T(2,128)} %rw_hbm.1, f32[2,4096]{1,0:T(2,128)} %cw_hbm.1, s32[1024]{0:T(1024)} %waves_ref.1, s32[8,128]{1,0:T(8,128)} %bitcast.10, ...), custom_call_target="tpu_custom_call" | custom-call | tf_op jit(solution)/shard_map/model_step/pallas_call | solution.py:523
  44.9 1.9 %copy.15 = bf16[16,2,4096]{2,1,0:T(2,128)(2,1)} copy(bf16[16,2,4096]{2,0,1:T(8,128)(2,1)} %bitcast.7) | data formatting | bytes 524288 | tf_op jit(solution)/shard_map/transpose | solution.py:568

commit v3 on v2

--- a/solution.py
+++ b/solution.py
@@ -123,8 +123,8 @@
     return north, permuted(turn, south).astype(BF16)
 
 
-def interpolate(start, sources, row_ref, col_ref, rw_ref, cw_ref, departed_ref):
-    levels, lon = departed_ref.shape[1:]
+def departure_weights(start, row_ref, col_ref, rw_ref, cw_ref, near_ref, col_w_ref, far_ref):
+    lon = row_ref.shape[1]
     sub = lax.broadcasted_iota(jnp.int32, (8, lon), 0) - 2
     lon_ids = lax.broadcasted_iota(jnp.int32, (1, lon), 1)
     for i in range(2):
@@ -134,20 +134,41 @@
         b = cw_ref[i : i + 1, :]
         row_w = jnp.where(rel_row == sub, 1.0 - a, 0.0) + jnp.where(rel_row == sub - 1, a, 0.0)
         col_w = jnp.where(rel_col == sub, 1.0 - b, 0.0) + jnp.where(rel_col == sub - 1, b, 0.0)
-        shifted = [
-            row_w if dc == 0 else pltpu.roll(row_w, dc % lon, 1) for dc in range(-2, 4)
-        ]
+        for dc in range(-2, 4):
+            near_ref[i, dc + 2] = row_w if dc == 0 else pltpu.roll(row_w, dc % lon, 1)
+        col_w_ref[i] = col_w
+        far_ref[i] = row_w[4 * i : 4 * i + 1, :] * col_w
+
+
+def near_rows(sources, near_ref, col_w_ref, departed_ref):
+    levels, lon = departed_ref.shape[1:]
+    for i in range(2):
         for h in range(levels // 8):
             total = None
             for dc in range(-2, 4):
                 mixed = None
-                for dr in range(5):
-                    term = shifted[dc + 2][dr : dr + 1, :] * sources[i + dr, 8 * h : 8 * h + 8, :]
+                for dr in range(1 - i, 5 - i):
+                    term = (
+                        near_ref[i, dc + 2, dr : dr + 1, :]
+                        * sources[i + dr - 1, 8 * h : 8 * h + 8, :]
+                    )
                     mixed = term if mixed is None else mixed + term
                 if dc != 0:
                     mixed = pltpu.roll(mixed, (-dc) % lon, 1)
-                term = col_w[dc + 2 : dc + 3, :] * mixed
+                term = col_w_ref[i, dc + 2 : dc + 3, :] * mixed
                 total = term if total is None else total + term
+            departed_ref[i, 8 * h : 8 * h + 8, :] = total
+
+
+def far_rows(rows, far_ref, departed_ref):
+    levels, lon = departed_ref.shape[1:]
+    for i in range(2):
+        for h in range(levels // 8):
+            source = rows[i][8 * h : 8 * h + 8, :].astype(F32)
+            total = departed_ref[i, 8 * h : 8 * h + 8, :]
+            for dc in range(-2, 4):
+                moved = source if dc == 0 else pltpu.roll(source, (-dc) % lon, 1)
+                total = total + far_ref[i, dc + 2 : dc + 3, :] * moved
             departed_ref[i, 8 * h : 8 * h + 8, :] = total
 
 
@@ -343,7 +364,7 @@
     gamma_ref, place_hbm, optics_hbm, kabs_hbm, planck_hbm, kdown_hbm, out_ref,
     row_ref, col_ref, rw_ref, cw_ref, wave_tile_ref, legendre_ref, place_ref, optics_ref,
     kabs_ref, planck_ref, kdown_ref,
-    before, after, sources, departed, table, tall_ref, z_ref, ft_ref, mix_ref, e_ref, optics_all,
+    before, after, sources, near_ref, col_w_ref, far_ref, departed, table, tall_ref, z_ref, ft_ref, mix_ref, e_ref, optics_all,
     sent, got, answer, back,
     load_sems, halo_send, halo_recv, opt_send, opt_recv, relay_send, relay_recv,
     out_send, out_recv, back_send, back_recv, ready,
@@ -385,7 +406,7 @@
         )
 
     for i in range(2):
-        sources[2 + i] = own_ref[i].astype(F32)
+        sources[1 + i] = own_ref[i].astype(F32)
     loads[0].wait()
     rows = slot_waves(wave_tile_ref[...])
     fold = fold_of(rows)
@@ -394,14 +415,17 @@
 
     pl.semaphore_wait(barrier, 40)
 
-    halo = [
-        pltpu.make_async_remote_copy(
-            src_ref=own_ref, dst_ref=target, send_sem=halo_send.at[n], recv_sem=halo_recv.at[n],
+    def halo(n, row):
+        other, target = ((following, before), (previous, after))[n]
+        return pltpu.make_async_remote_copy(
+            src_ref=own_ref.at[row], dst_ref=target.at[row],
+            send_sem=halo_send.at[2 * n + row], recv_sem=halo_recv.at[2 * n + row],
             device_id=(other // 32, lax.rem(other, 32)), device_id_type=MESH,
         )
-        for n, (other, target) in enumerate(((following, before), (previous, after)))
-    ]
-    for move in halo:
+
+    near = (halo(0, 1), halo(1, 0))
+    far = (halo(0, 0), halo(1, 1))
+    for move in near + far:
         move.start()
 
     @pl.loop(1, 8)
@@ -421,10 +445,6 @@
             send_sem=opt_send.at[k], recv_sem=opt_recv.at[k],
             device_id=(g, peer * 2 + core), device_id_type=MESH,
         )
-
-    @pl.loop(1, 16)
-    def _(k):
-        optics_copy(k, lax.rem(chip + k, 16), chip).start()
 
     optics_all[optics_rows(chip), :] = optics_ref[...]
     temps = coarse_means(own_ref)
@@ -455,12 +475,22 @@
 
     for load in loads[2:6]:
         load.wait()
-    for move in halo:
+    departure_weights(
+        2 * me, row_ref, col_ref, rw_ref, cw_ref, near_ref, col_w_ref, far_ref
+    )
+    for move in near:
         move.wait_recv()
-    for i in range(2):
-        sources[i] = before[i].astype(F32)
-        sources[4 + i] = after[i].astype(F32)
-    interpolate(2 * me, sources, row_ref, col_ref, rw_ref, cw_ref, departed)
+    sources[0] = before[1].astype(F32)
+    sources[3] = after[0].astype(F32)
+    near_rows(sources, near_ref, col_w_ref, departed)
+    for move in far:
+        move.wait_recv()
+
+    @pl.loop(1, 16)
+    def _(k):
+        optics_copy(k, lax.rem(chip + k, 16), chip).start()
+
+    far_rows((before.at[0], after.at[1]), far_ref, departed)
     forward_waves(departed, z_ref, tall_ref, fold, ft_ref, mix_ref, sent)
     pl.semaphore_wait(ready, 7)
 
@@ -481,25 +511,26 @@
     relay_copy(core).start()
     turn = one_hot((256, 256), lambda row: 255 - row)
     gamma = level_column(gamma_ref, 2 * levels)
-    for load in loads[6:]:
+    loads[6].wait()
+    outward.wait_recv()
+    north, south = legendre_step(
+        got[0:128].reshape(256, 128), got[128:256].reshape(256, 128), legendre_ref, gamma,
+        waves_ref, me * 4, turn, trunc,
+    )
+    answer[0:128] = north.reshape(128, 2, 128)
+    answer[128:256] = south.reshape(128, 2, 128)
+    homeward = exchange(answer, back, back_send, back_recv)
+    for load in loads[7:]:
         load.wait()
     relay_copy(1 - core).wait_recv()
     heat = radiate(
         temps, place_ref[...], optics_all, tall(kabs_ref[...]), tall(planck_ref[...]),
         kdown_ref[...],
     )
-    outward.wait_recv()
-    north, south = legendre_step(
-        got[0:128].reshape(256, 128), got[128:256].reshape(256, 128), legendre_ref, gamma,
-        waves_ref, me * 4, turn, trunc,
-    )
-    answer[0:128] = north.reshape(128, 2, 128)
-    answer[128:256] = south.reshape(128, 2, 128)
-    homeward = exchange(answer, back, back_send, back_recv)
     heat = spread_heat(heat, lon)
     homeward.wait_recv()
     inverse_waves(back, table, fold, heat, e_ref, mix_ref, out_ref)
-    for move in halo:
+    for move in near + far:
         move.wait_send()
     relay_copy(core).wait_send()
     outward.wait_send()
@@ -542,7 +573,10 @@
             pltpu.VMEM((levels, 128), F32),
             pltpu.VMEM((lat_rows, levels, lon), BF16),
             pltpu.VMEM((lat_rows, levels, lon), BF16),
-            pltpu.VMEM((6, levels, lon), F32),
+            pltpu.VMEM((4, levels, lon), F32),
+            pltpu.VMEM((2, 6, 8, lon), F32),
+            pltpu.VMEM((2, 8, lon), F32),
+            pltpu.VMEM((2, 8, lon), F32),
             pltpu.VMEM((2, levels, lon), F32),
             pltpu.VMEM((2048, 256), BF16),
             pltpu.VMEM((8, 256, 256), BF16),
@@ -553,7 +587,7 @@
             pltpu.VMEM((owners * levels, coarse), BF16),
         ]
         + [pltpu.VMEM((groups * owners, 2, 128), BF16)] * 4
-        + [dma((11,)), dma((2,)), dma((2,)), dma((16,)), dma((16,)), dma((1,)), dma((1,))]
+        + [dma((11,)), dma((4,)), dma((4,)), dma((16,)), dma((16,)), dma((1,)), dma((1,))]
         + [dma((1,))] * 4
         + [pltpu.SemaphoreType.REGULAR],
         compiler_params=pltpu.CompilerParams(

time: 47 us -> 44.1 us (0.938)
  Pallas kernels: 43.1 us -> 40.2 us
    pallas_call x1, Pallas kernels: 43.1 us -> 40.2 us  [shards(): pl.pallas_call(functools.partial(step_kernel, trunc), out_shape=jax.Shape...]
where the time goes in v3:
time: 44.1 us; the launch traced here: 44 us
  Pallas kernels  40.2 us (91%)
  local copies, waits for them, and re-layouts  3.73 us (8%)
    pallas_call x1, Pallas kernels, shards(): pl.pallas_call(functools.partial(step_kernel, trunc), out_shape=jax.Shape...  40.2 us
    transpose x1, local copies, waits for them, and re-layouts, shards(): return jnp.transpose(result, (1, 0, 2))  1.93 us
    unnamed x1, local copies, waits for them, and re-layouts  1.8 us

profile of v3, /device:TPU:1, one launch (start us, length us, event | category | flops | bytes accessed | tf_op | source)
XLA Modules:
  0.0 44.0 jit_solution(10831564895969123006)
XLA Ops:
  0.0 1.8 %copy.17 = bf16[16,2,4096]{2,0,1:T(8,128)(2,1)} copy(bf16[16,2,4096]{2,1,0:T(2,128)(2,1)} %param.13) | data formatting | bytes 524288 | tf_op args[0]
  1.8 40.2 %model_step.1 = bf16[2,16,4096]{2,1,0:T(8,128)(2,1)} custom-call(bf16[2,16,4096]{2,1,0:T(8,128)(2,1)} %bitcast.8, s32[2,4096]{1,0:T(2,128)} %row_hbm.1, s32[2,4096]{1,0:T(2,128)} %col_hbm.1, f32[2,4096]{1,0:T(2,128)} %rw_hbm.1, f32[2,4096]{1,0:T(2,128)} %cw_hbm.1, s32[1024]{0:T(1024)} %waves_ref.1, s32[8,128]{1,0:T(8,128)} %bitcast.10, ...), custom_call_target="tpu_custom_call" | custom-call | tf_op jit(solution)/shard_map/model_step/pallas_call | solution.py:554
  42.1 1.9 %copy.15 = bf16[16,2,4096]{2,1,0:T(2,128)(2,1)} copy(bf16[16,2,4096]{2,0,1:T(8,128)(2,1)} %bitcast.7) | data formatting | bytes 524288 | tf_op jit(solution)/shard_map/transpose | solution.py:602

commit v4 on v3

--- a/solution.py
+++ b/solution.py
@@ -360,11 +360,11 @@
 
 
 def step_kernel(
-    trunc, own_ref, row_hbm, col_hbm, rw_hbm, cw_hbm, waves_ref, wave_tile_hbm, legendre_hbm,
+    trunc, state_hbm, row_hbm, col_hbm, rw_hbm, cw_hbm, waves_ref, wave_tile_hbm, legendre_hbm,
     gamma_ref, place_hbm, optics_hbm, kabs_hbm, planck_hbm, kdown_hbm, out_ref,
     row_ref, col_ref, rw_ref, cw_ref, wave_tile_ref, legendre_ref, place_ref, optics_ref,
     kabs_ref, planck_ref, kdown_ref,
-    before, after, sources, near_ref, col_w_ref, far_ref, departed, table, tall_ref, z_ref, ft_ref, mix_ref, e_ref, optics_all,
+    raw_ref, own_ref, before, after, sources, near_ref, col_w_ref, far_ref, departed, table, tall_ref, z_ref, ft_ref, mix_ref, e_ref, optics_all,
     sent, got, answer, back,
     load_sems, halo_send, halo_recv, opt_send, opt_recv, relay_send, relay_recv,
     out_send, out_recv, back_send, back_recv, ready,
@@ -377,12 +377,12 @@
         (wave_tile_hbm, wave_tile_ref), (optics_hbm, optics_ref),
         (row_hbm, row_ref), (col_hbm, col_ref), (rw_hbm, rw_ref), (cw_hbm, cw_ref),
         (legendre_hbm, legendre_ref), (place_hbm, place_ref), (kabs_hbm, kabs_ref),
-        (planck_hbm, planck_ref), (kdown_hbm, kdown_ref),
+        (planck_hbm, planck_ref), (kdown_hbm, kdown_ref), (state_hbm, raw_ref),
     )
     loads = [
         pltpu.make_async_copy(src, dst, load_sems.at[n]) for n, (src, dst) in enumerate(moves)
     ]
-    for load in loads:
+    for load in loads[-1:] + loads[:-1]:
         load.start()
 
     barrier = pltpu.get_barrier_semaphore()
@@ -405,8 +405,13 @@
             barrier, inc=1, device_id=(lax.rem(g + k, 8), a), device_id_type=MESH
         )
 
-    for i in range(2):
-        sources[1 + i] = own_ref[i].astype(F32)
+    loads[-1].wait()
+    for n in range(lon // 512):
+        part = slice(512 * n, 512 * n + 512)
+        block = raw_ref[:, :, part].astype(F32)
+        for i in range(2):
+            sources[1 + i, :, part] = block[:, i, :]
+            own_ref[i, :, part] = block[:, i, :].astype(BF16)
     loads[0].wait()
     rows = slot_waves(wave_tile_ref[...])
     fold = fold_of(rows)
@@ -520,7 +525,7 @@
     answer[0:128] = north.reshape(128, 2, 128)
     answer[128:256] = south.reshape(128, 2, 128)
     homeward = exchange(answer, back, back_send, back_recv)
-    for load in loads[7:]:
+    for load in loads[7:11]:
         load.wait()
     relay_copy(1 - core).wait_recv()
     heat = radiate(
@@ -546,7 +551,6 @@
     groups = lax.axis_size("grp")
     trunc = wave_of.shape[0] - 1
     coarse = lon // 4
-    own = jnp.transpose(state, (1, 0, 2))
     in_vmem = pl.BlockSpec(memory_space=pltpu.VMEM)
     in_smem = pl.BlockSpec(memory_space=pltpu.SMEM)
     in_hbm = pl.BlockSpec(memory_space=pltpu.HBM)
@@ -555,7 +559,7 @@
         functools.partial(step_kernel, trunc),
         out_shape=jax.ShapeDtypeStruct((lat_rows, levels, lon), BF16),
         in_specs=[
-            in_vmem, in_hbm, in_hbm, in_hbm, in_hbm, in_smem, in_hbm, in_hbm,
+            in_hbm, in_hbm, in_hbm, in_hbm, in_hbm, in_smem, in_hbm, in_hbm,
             in_smem, in_hbm, in_hbm, in_hbm, in_hbm, in_hbm,
         ],
         out_specs=in_vmem,
@@ -571,6 +575,8 @@
             pltpu.VMEM((levels, 128), F32),
             pltpu.VMEM((levels, 128), F32),
             pltpu.VMEM((levels, 128), F32),
+            pltpu.VMEM((levels, lat_rows, lon), BF16),
+            pltpu.VMEM((lat_rows, levels, lon), BF16),
             pltpu.VMEM((lat_rows, levels, lon), BF16),
             pltpu.VMEM((lat_rows, levels, lon), BF16),
             pltpu.VMEM((4, levels, lon), F32),
@@ -587,7 +593,7 @@
             pltpu.VMEM((owners * levels, coarse), BF16),
         ]
         + [pltpu.VMEM((groups * owners, 2, 128), BF16)] * 4
-        + [dma((11,)), dma((4,)), dma((4,)), dma((16,)), dma((16,)), dma((1,)), dma((1,))]
+        + [dma((12,)), dma((4,)), dma((4,)), dma((16,)), dma((16,)), dma((1,)), dma((1,))]
         + [dma((1,))] * 4
         + [pltpu.SemaphoreType.REGULAR],
         compiler_params=pltpu.CompilerParams(
@@ -595,7 +601,7 @@
         ),
         name="model_step",
     )(
-        own, dep_row, dep_col, row_weight, col_weight, wave_of,
+        state, dep_row, dep_col, row_weight, col_weight, wave_of,
         wave_of.reshape(groups, owners * 4), legendre, gamma, rad_place,
         jnp.transpose(optics), kabs, planck_weight, jnp.transpose(kdown),
     )

time: 44.1 us -> 41.9 us (0.950)
  local copies, waits for them, and re-layouts: 3.73 us -> 1.93 us
    unnamed x1 -> x0, local copies, waits for them, and re-layouts: 1.8 us -> none
where the time goes in v4:
time: 41.9 us; the launch traced here: 41.8 us
  Pallas kernels  39.8 us (95%)
  local copies, waits for them, and re-layouts  1.93 us (5%)
    pallas_call x1, Pallas kernels, shards(): pl.pallas_call(functools.partial(step_kernel, trunc), out_shape=jax.Shape...  39.8 us
    transpose x1, local copies, waits for them, and re-layouts, shards(): return jnp.transpose(result, (1, 0, 2))  1.93 us

profile of v4, /device:TPU:1, one launch (start us, length us, event | category | flops | bytes accessed | tf_op | source)
XLA Modules:
  0.0 41.8 jit_solution(2980467007793676938)
XLA Ops:
  0.0 39.8 %model_step.1 = bf16[2,16,4096]{2,1,0:T(8,128)(2,1)} custom-call(bf16[16,2,4096]{2,1,0:T(2,128)(2,1)} %state_hbm.1, s32[2,4096]{1,0:T(2,128)} %row_hbm.1, s32[2,4096]{1,0:T(2,128)} %col_hbm.1, f32[2,4096]{1,0:T(2,128)} %rw_hbm.1, f32[2,4096]{1,0:T(2,128)} %cw_hbm.1, s32[1024]{0:T(1024)} %waves_ref.1, s32[8,128]{1,0:T(8,128)} %bitcast.6, ...), custom_call_target="tpu_custom_call" | custom-call | tf_op jit(solution)/shard_map/model_step/pallas_call | solution.py:558
  39.8 1.9 %copy.14 = bf16[16,2,4096]{2,1,0:T(2,128)(2,1)} copy(bf16[16,2,4096]{2,0,1:T(8,128)(2,1)} %bitcast.4) | data formatting | bytes 524288 | tf_op jit(solution)/shard_map/transpose | solution.py:608

commit v5 on v4

--- a/solution.py
+++ b/solution.py
@@ -465,7 +465,7 @@
 
         @pl.loop(0, 7)
         def _(k):
-            z = g ^ jnp.where(k < 4, 4 + k, 7 - k)
+            z = g ^ jnp.where(k < 2, 4 + k, jnp.where(k == 2, 3, jnp.where(k < 5, 10 - k, 7 - k)))
             for step in LAT_STEPS:
                 send(z, a ^ step)
 

time: 41.9 us -> 42.6 us (1.017)
  Pallas kernels: 39.8 us -> 40.5 us
    pallas_call x1, Pallas kernels: 39.8 us -> 40.5 us  [shards(): pl.pallas_call(functools.partial(step_kernel, trunc), out_shape=jax.Shape...]
where the time goes in v5:
time: 42.6 us; the launch traced here: 42.5 us
  Pallas kernels  40.5 us (95%)
  local copies, waits for them, and re-layouts  1.93 us (5%)
    pallas_call x1, Pallas kernels, shards(): pl.pallas_call(functools.partial(step_kernel, trunc), out_shape=jax.Shape...  40.5 us
    transpose x1, local copies, waits for them, and re-layouts, shards(): return jnp.transpose(result, (1, 0, 2))  1.93 us

profile of v5, /device:TPU:1, one launch (start us, length us, event | category | flops | bytes accessed | tf_op | source)
XLA Modules:
  0.0 42.5 jit_solution(17144347846344442062)
XLA Ops:
  0.0 40.5 %model_step.1 = bf16[2,16,4096]{2,1,0:T(8,128)(2,1)} custom-call(bf16[16,2,4096]{2,1,0:T(2,128)(2,1)} %state_hbm.1, s32[2,4096]{1,0:T(2,128)} %row_hbm.1, s32[2,4096]{1,0:T(2,128)} %col_hbm.1, f32[2,4096]{1,0:T(2,128)} %rw_hbm.1, f32[2,4096]{1,0:T(2,128)} %cw_hbm.1, s32[1024]{0:T(1024)} %waves_ref.1, s32[8,128]{1,0:T(8,128)} %bitcast.6, ...), custom_call_target="tpu_custom_call" | custom-call | tf_op jit(solution)/shard_map/model_step/pallas_call | solution.py:558
  40.5 1.9 %copy.14 = bf16[16,2,4096]{2,1,0:T(2,128)(2,1)} copy(bf16[16,2,4096]{2,0,1:T(8,128)(2,1)} %bitcast.4) | data formatting | bytes 524288 | tf_op jit(solution)/shard_map/transpose | solution.py:608
